TPU v7x, 256 devices: a whole 4x4x8 slice. The times are simulated.
256 devices in a mesh: tm: 8 (over z), gx: 8 (over x, core), gy: 4 (over y).
Axes of the slice: x: 4, y: 4, z: 8, core: 2. Of those that a mesh axis runs over, the one named last changes fastest.
Arguments:
- state_starts: float32 [8, 64, 256, 512], P('tm', None, 'gx', 'gy'), may hold values from -4 to 4, as said below
- diffusivity: float32 [64], replicated, may hold values from 0.3 to 1.2
- wind: float32 [2, 64], replicated, may hold values from -0.6 to 0.6
Outputs:
- segment_ends: float32 [8, 64, 256, 512], P('tm', None, 'gx', 'gy')
Inputs may be any that keep to these rules, and one draw needn't show every extreme that they name: `state_starts`: states of order one.
All inputs are finite; a program needn't handle non-finite values.
Results may differ from a plain program's by a relative error of at most 0.0001.
Values sent between devices are 32-bit elements; how exact they have to be, the bound alone decides.
No kernel may reach another device: no remote copies, remote signals or barrier semaphores. Data moves between devices by JAX's collectives and lax.ppermute only.
A program may use at most 64 MiB of HBM per device.

v0:
```python
import jax
import jax.numpy as jnp
from jax import lax
from jax.sharding import PartitionSpec as P

SUB = 4


time_step = 0.2
weights_low = (0.375, 0.125, 0.0, 0.0)
weights_mid = (0.625, 0.875, 0.875, 0.625)
weights_high = (0.0, 0.0, 0.125, 0.375)


def extended(array, sides, width):
    for axis, dim in sides:
        devices, length = (lax.axis_size(axis), array.shape[dim])
        up = [(i, (i + 1) % devices) for i in range(devices - 1)]
        down = [(j, i) for i, j in up]
        last = lax.slice_in_dim(array, length - width, length, axis=dim)
        leading = lax.slice_in_dim(array, 0, width, axis=dim)
        before = lax.ppermute(last, axis, up)
        after = lax.ppermute(leading, axis, down)
        array = jnp.concatenate([before, array, after], axis=dim)
    return array


def passed_along(block, axis, distance):
    devices = range(lax.axis_size(axis))
    route = [(i - distance, i) for i in devices if i - distance in devices]
    return lax.ppermute(block, axis, route)


def advance(padded, diffuse, wind_east, wind_north, factor):
    centre = padded[:, 1:-1, 1:-1]
    east = padded[:, 2:, 1:-1]
    west = padded[:, :-2, 1:-1]
    north = padded[:, 1:-1, 2:]
    south = padded[:, 1:-1, :-2]
    laplace = east + west + north + south - 4.0 * centre
    slope = wind_east * (east - west) * 0.5 + wind_north * (north - south) * 0.5
    return centre + time_step * (factor * diffuse * laplace - centre * slope)


def restrict(field):
    levels, rows, cols = field.shape
    return field.reshape(levels, rows // 4, 4, cols // 4, 4).mean(axis=(2, 4))


def prolong(padded):
    levels, rows_ext, cols_ext = padded.shape
    coarse_rows = rows_ext - 2
    coarse_cols = cols_ext - 2
    parts = [
        weights_low[offset] * padded[:, :-2, :]
        + weights_mid[offset] * padded[:, 1:-1, :]
        + weights_high[offset] * padded[:, 2:, :]
        for offset in range(4)
    ]
    along = jnp.stack(parts, axis=2).reshape(levels, 4 * coarse_rows, cols_ext)
    parts = [
        weights_low[offset] * along[:, :, :-2]
        + weights_mid[offset] * along[:, :, 1:-1]
        + weights_high[offset] * along[:, :, 2:]
        for offset in range(4)
    ]
    return jnp.stack(parts, axis=3).reshape(levels, 4 * coarse_rows, 4 * coarse_cols)


def shards(state_starts, diffusivity, wind):
    begin = state_starts[0]
    diffuse = diffusivity[:, None, None]
    wind_east = wind[0][:, None, None]
    wind_north = wind[1][:, None, None]
    field = begin
    for substep in range(SUB):
        padded = extended(field, (("gx", 1), ("gy", 2)), 1)
        field = advance(padded, diffuse, wind_east, wind_north, 1.0)
    fine_end = field
    coarse_begin = restrict(begin)

    def propagate(coarse):
        padded = extended(coarse, (("gx", 1), ("gy", 2)), 1)
        return advance(padded, diffuse, wind_east, wind_north, 0.25)

    old_image = propagate(coarse_begin)

    def padded_change(coarse):
        change = propagate(coarse) - old_image
        return extended(change, (("gx", 1), ("gy", 2)), 1)

    first_segment = lax.axis_index("tm") == 0

    def next_coarse(coarse):
        return restrict(fine_end + prolong(padded_change(coarse)))

    def one_turn(turn_index, coarse):
        passed = passed_along(next_coarse(coarse), "tm", 1)
        return jnp.where(first_segment, coarse, passed)

    coarse_final = lax.fori_loop(0, lax.axis_size("tm") - 1, one_turn, coarse_begin)
    ending = fine_end + prolong(padded_change(coarse_final))
    return ending[None]


def solution(mesh):
    placed = (P("tm", None, "gx", "gy"), P(), P())
    return jax.shard_map(
        shards, mesh=mesh, in_specs=placed, out_specs=P("tm", None, "gx", "gy"), check_vma=False
    )
```

profile of v0, /device:TPU:1, one launch (start us, length us, event | category | flops | bytes accessed | tf_op | source)
XLA Modules:
  0.0 455.3 jit_solution(8514936725151694837)
XLA Ops:
  3.2 4.5 collective-permute-start.10
  14.6 4.0 collective-permute-start.12
  19.5 8.5 %multiply_add_fusion.5 = f32[64,32,128]{0,1,2:T(8,128)S(1)} fusion(f32[64,32,128]{0,1,2:T(8,128)} %bitcast.77, f32[64,1,128]{0,1,2:T(1,128)S(1)} %collective-permute-done.9, f32[64,1,128]{0,1,2:T(1,128)S(1)} %collective-permute-done.10, f32[64,34,1]{0,1,2:T(8,128)S(1)} %collective-permute-done.12, f32[64,34,1]{0,1,2:T(8,128)S(1)} %collective-permute-done.11, ...), kind=kLoop, calls=%fused_computation.67 | loop fusion | flops 6291456 | bytes 2180864 | tf_op jit(solution)/shard_map/add | solution.py:42
  38.7 4.6 %collective-permute-start.16 = (f32[64,34,1]{0,1,2:T(8,128)S(1)}, f32[64,34,1]{0,1,2:T(8,128)S(1)}, u32[]{:S(2)}, u32[]{:S(2)}) collective-permute-start(f32[64,34,1]{0,1,2:T(8,128)S(1)} %get-tuple-element.109), channel_id=1, source_target_pairs={{0,1},{1,2},{2,3},{4,5},{5,6},{6,7},{8,9},{9,10},{10,11},{12,13},{... | collective-permute-start | bytes 26120 | tf_op jit(solution)/shard_map/ppermute | solution.py:22
  44.2 8.4 %multiply_add_fusion.4 = f32[64,32,128]{0,1,2:T(8,128)S(1)} fusion(f32[64,32,128]{0,1,2:T(8,128)} %copy-done.2, f32[64,1,128]{0,1,2:T(1,128)S(1)} %collective-permute-done.13, f32[64,1,128]{0,1,2:T(1,128)S(1)} %collective-permute-done.14, f32[64,34,1]{0,1,2:T(8,128)S(1)} %collective-permute-done.16, f32[64,34,1]{0,1,2:T(8,128)S(1)} %collective-permute-done.15, ...), kind=kLoop, calls=%fused_computation.66 | loop fusion | flops 6291456 | bytes 2180864 | tf_op jit(solution)/shard_map/add | solution.py:42
  52.7 4.5 collective-permute-start.18
  66.1 4.6 %collective-permute-start.20 = (f32[64,34,1]{0,1,2:T(8,128)S(1)}, f32[64,34,1]{0,1,2:T(8,128)S(1)}, u32[]{:S(2)}, u32[]{:S(2)}) collective-permute-start(f32[64,34,1]{0,1,2:T(8,128)S(1)} %get-tuple-element.107), channel_id=1, source_target_pairs={{0,1},{1,2},{2,3},{4,5},{5,6},{6,7},{8,9},{9,10},{10,11},{12,13},{... | collective-permute-start | bytes 26120 | tf_op jit(solution)/shard_map/ppermute | solution.py:22
  75.2 4.5 collective-permute-start.22
  83.0 4.6 %collective-permute-start.28 = (f32[64,10,1]{0,2,1:T(1,128)S(1)}, f32[64,10,1]{0,2,1:T(1,128)S(1)}, u32[]{:S(2)}, u32[]{:S(2)}) collective-permute-start(f32[64,10,1]{0,2,1:T(1,128)S(1)} %get-tuple-element.133), channel_id=1, source_target_pairs={{0,1},{1,2},{2,3},{4,5},{5,6},{6,7},{8,9},{9,10},{10,11},{12,13},{... | collective-permute-start | bytes 7688 | tf_op jit(solution)/shard_map/ppermute | solution.py:22
  88.9 4.5 collective-permute-start.24
  98.9 314.0 %while.10 = (s32[]{:T(128)}, f32[64,8,32]{0,2,1:T(8,128)S(1)}, pred[]{:T(512)}, f32[64,32,128]{0,2,1:T(8,128)S(1)}, f32[64,1,1]{0,2,1:T(1,128)S(1)}, /*index=5*/...) while((s32[]{:T(128)}, f32[64,8,32]{0,2,1:T(8,128)S(1)}, ...), condition=%wide.region_3.4_spmd, body=%wide.region_1.3_spmd.sunk | while | flops 3296834 | bytes 9416390 | solution.py:101
  98.9 4.8 %collective-permute-start = (f32[64,1,32]{0,2,1:T(8,128)S(1)}, f32[64,1,32]{0,2,1:T(8,128)S(1)}, u32[]{:S(2)}, u32[]{:S(2)}) collective-permute-start(f32[64,1,32]{0,2,1:T(8,128)S(1)} %get-tuple-element.209), channel_id=1, source_target_pairs={{0,4},{4,8},{8,12},{12,16},{16,20},{20,24},{24,28},{1,5},{5,9},{9,... | collective-permute-start | bytes 24584 | tf_op jit(solution)/shard_map/while/body/eval_jaxpr/ppermute | solution.py:22
  125.2 4.3 collective-permute-start.7
  143.3 4.6 %collective-permute-start = (f32[64,1,32]{0,2,1:T(8,128)S(1)}, f32[64,1,32]{0,2,1:T(8,128)S(1)}, u32[]{:S(2)}, u32[]{:S(2)}) collective-permute-start(f32[64,1,32]{0,2,1:T(8,128)S(1)} %get-tuple-element.209), channel_id=1, source_target_pairs={{0,4},{4,8},{8,12},{12,16},{16,20},{20,24},{24,28},{1,5},{5,9},{9,... | collective-permute-start | bytes 24584 | tf_op jit(solution)/shard_map/while/body/eval_jaxpr/ppermute | solution.py:22
  169.4 4.0 collective-permute-start.7
  180.3 4.1 collective-permute-start.8
  187.4 5.2 %collective-permute-start = (f32[64,1,32]{0,2,1:T(8,128)S(1)}, f32[64,1,32]{0,2,1:T(8,128)S(1)}, u32[]{:S(2)}, u32[]{:S(2)}) collective-permute-start(f32[64,1,32]{0,2,1:T(8,128)S(1)} %get-tuple-element.209), channel_id=1, source_target_pairs={{0,4},{4,8},{8,12},{12,16},{16,20},{20,24},{24,28},{1,5},{5,9},{9,... | collective-permute-start | bytes 24584 | tf_op jit(solution)/shard_map/while/body/eval_jaxpr/ppermute | solution.py:22
  213.8 4.0 collective-permute-start.7
  224.8 4.1 collective-permute-start.8
  231.9 5.2 %collective-permute-start = (f32[64,1,32]{0,2,1:T(8,128)S(1)}, f32[64,1,32]{0,2,1:T(8,128)S(1)}, u32[]{:S(2)}, u32[]{:S(2)}) collective-permute-start(f32[64,1,32]{0,2,1:T(8,128)S(1)} %get-tuple-element.209), channel_id=1, source_target_pairs={{0,4},{4,8},{8,12},{12,16},{16,20},{20,24},{24,28},{1,5},{5,9},{9,... | collective-permute-start | bytes 24584 | tf_op jit(solution)/shard_map/while/body/eval_jaxpr/ppermute | solution.py:22
  258.3 4.0 collective-permute-start.7
  269.2 4.1 collective-permute-start.8
  276.3 5.2 %collective-permute-start = (f32[64,1,32]{0,2,1:T(8,128)S(1)}, f32[64,1,32]{0,2,1:T(8,128)S(1)}, u32[]{:S(2)}, u32[]{:S(2)}) collective-permute-start(f32[64,1,32]{0,2,1:T(8,128)S(1)} %get-tuple-element.209), channel_id=1, source_target_pairs={{0,4},{4,8},{8,12},{12,16},{16,20},{20,24},{24,28},{1,5},{5,9},{9,... | collective-permute-start | bytes 24584 | tf_op jit(solution)/shard_map/while/body/eval_jaxpr/ppermute | solution.py:22
  302.7 4.0 collective-permute-start.7
  313.7 4.9 %collective-permute-start.8 = (f32[64,8,32]{0,2,1:T(8,128)S(1)}, f32[64,8,32]{0,2,1:T(8,128)S(1)}, u32[]{:S(2)}, u32[]{:S(2)}) collective-permute-start(f32[64,8,32]{0,2,1:T(8,128)S(1)} %broadcast_multiply_fusion.4), channel_id=1, source_target_pairs={{0,32},{32,64},{64,96},{96,128},{128,160},{160,192},{192,224},{1,3... | collective-permute-start | bytes 196616 | tf_op jit(solution)/shard_map/while/body/eval_jaxpr/ppermute | solution.py:31
  321.6 5.2 %collective-permute-start = (f32[64,1,32]{0,2,1:T(8,128)S(1)}, f32[64,1,32]{0,2,1:T(8,128)S(1)}, u32[]{:S(2)}, u32[]{:S(2)}) collective-permute-start(f32[64,1,32]{0,2,1:T(8,128)S(1)} %get-tuple-element.209), channel_id=1, source_target_pairs={{0,4},{4,8},{8,12},{12,16},{16,20},{20,24},{24,28},{1,5},{5,9},{9,... | collective-permute-start | bytes 24584 | tf_op jit(solution)/shard_map/while/body/eval_jaxpr/ppermute | solution.py:22
  348.0 4.0 collective-permute-start.7
  358.9 5.3 %collective-permute-start.8 = (f32[64,8,32]{0,2,1:T(8,128)S(1)}, f32[64,8,32]{0,2,1:T(8,128)S(1)}, u32[]{:S(2)}, u32[]{:S(2)}) collective-permute-start(f32[64,8,32]{0,2,1:T(8,128)S(1)} %broadcast_multiply_fusion.4), channel_id=1, source_target_pairs={{0,32},{32,64},{64,96},{96,128},{128,160},{160,192},{192,224},{1,3... | collective-permute-start | bytes 196616 | tf_op jit(solution)/shard_map/while/body/eval_jaxpr/ppermute | solution.py:31
  367.2 5.2 %collective-permute-start = (f32[64,1,32]{0,2,1:T(8,128)S(1)}, f32[64,1,32]{0,2,1:T(8,128)S(1)}, u32[]{:S(2)}, u32[]{:S(2)}) collective-permute-start(f32[64,1,32]{0,2,1:T(8,128)S(1)} %get-tuple-element.209), channel_id=1, source_target_pairs={{0,4},{4,8},{8,12},{12,16},{16,20},{20,24},{24,28},{1,5},{5,9},{9,... | collective-permute-start | bytes 24584 | tf_op jit(solution)/shard_map/while/body/eval_jaxpr/ppermute | solution.py:22
  404.6 5.3 %collective-permute-start.8 = (f32[64,8,32]{0,2,1:T(8,128)S(1)}, f32[64,8,32]{0,2,1:T(8,128)S(1)}, u32[]{:S(2)}, u32[]{:S(2)}) collective-permute-start(f32[64,8,32]{0,2,1:T(8,128)S(1)} %broadcast_multiply_fusion.4), channel_id=1, source_target_pairs={{0,32},{32,64},{64,96},{96,128},{128,160},{160,192},{192,224},{1,3... | collective-permute-start | bytes 196616 | tf_op jit(solution)/shard_map/while/body/eval_jaxpr/ppermute | solution.py:31
  412.9 5.2 %collective-permute-start.30 = (f32[64,1,32]{0,2,1:T(8,128)S(1)}, f32[64,1,32]{0,2,1:T(8,128)S(1)}, u32[]{:S(2)}, u32[]{:S(2)}) collective-permute-start(f32[64,1,32]{0,2,1:T(8,128)S(1)} %get-tuple-element.137), channel_id=1, source_target_pairs={{0,4},{4,8},{8,12},{12,16},{16,20},{20,24},{24,28},{1,5},{5,9},{9,... | collective-permute-start | bytes 24584 | tf_op jit(solution)/shard_map/ppermute | solution.py:22
  424.4 4.5 collective-permute-start.32
  (351 shorter events, 303.5 us)
Async XLA Ops:
  3.2 6.5 %collective-permute-start.10 = (f32[64,1,128]{0,1,2:T(1,128)S(1)}, f32[64,1,128]{0,1,2:T(1,128)S(1)}, u32[]{:S(2)}, u32[]{:S(2)}) collective-permute-start(f32[64,1,128]{0,1,2:T(1,128)S(1)} %get-tuple-element.118), channel_id=1, source_target_pairs={{0,4},{4,8},{8,12},{12,16},{16,20},{20,24},{24,28},{1,5},{5,9},{9,... | collective-permute-start | bytes 98312 | tf_op jit(solution)/shard_map/ppermute | solution.py:22
  7.7 5.6 %collective-permute-start.9 = (f32[64,1,128]{0,1,2:T(1,128)S(1)}, f32[64,1,128]{0,1,2:T(1,128)S(1)}, u32[]{:S(2)}, u32[]{:S(2)}) collective-permute-start(f32[64,1,128]{0,1,2:T(1,128)S(1)} %get-tuple-element.119), channel_id=1, source_target_pairs={{4,0},{8,4},{12,8},{16,12},{20,16},{24,20},{28,24},{5,1},{9,5},{13... | collective-permute-start | bytes 98312 | tf_op jit(solution)/shard_map/ppermute | solution.py:23
  28.1 9.3 %collective-permute-start.14 = (f32[64,1,128]{0,1,2:T(1,128)S(1)}, f32[64,1,128]{0,1,2:T(1,128)S(1)}, u32[]{:S(2)}, u32[]{:S(2)}) collective-permute-start(f32[64,1,128]{0,1,2:T(1,128)S(1)} %get-tuple-element.116), channel_id=1, source_target_pairs={{0,4},{4,8},{8,12},{12,16},{16,20},{20,24},{24,28},{1,5},{5,9},{9,... | collective-permute-start | bytes 98312 | tf_op jit(solution)/shard_map/ppermute | solution.py:22
  31.1 6.3 %collective-permute-start.13 = (f32[64,1,128]{0,1,2:T(1,128)S(1)}, f32[64,1,128]{0,1,2:T(1,128)S(1)}, u32[]{:S(2)}, u32[]{:S(2)}) collective-permute-start(f32[64,1,128]{0,1,2:T(1,128)S(1)} %get-tuple-element.117), channel_id=1, source_target_pairs={{4,0},{8,4},{12,8},{16,12},{20,16},{24,20},{28,24},{5,1},{9,5},{13... | collective-permute-start | bytes 98312 | tf_op jit(solution)/shard_map/ppermute | solution.py:23
  37.4 5.9 %collective-permute-start.15 = (f32[64,34,1]{0,1,2:T(8,128)S(1)}, f32[64,34,1]{0,1,2:T(8,128)S(1)}, u32[]{:S(2)}, u32[]{:S(2)}) collective-permute-start(f32[64,34,1]{0,1,2:T(8,128)S(1)} %get-tuple-element.108), channel_id=1, source_target_pairs={{1,0},{2,1},{3,2},{5,4},{6,5},{7,6},{9,8},{10,9},{11,10},{13,12},{... | collective-permute-start | bytes 26120 | tf_op jit(solution)/shard_map/ppermute | solution.py:23
  52.7 12.0 %collective-permute-start.18 = (f32[64,1,128]{0,1,2:T(1,128)S(1)}, f32[64,1,128]{0,1,2:T(1,128)S(1)}, u32[]{:S(2)}, u32[]{:S(2)}) collective-permute-start(f32[64,1,128]{0,1,2:T(1,128)S(1)} %get-tuple-element.114), channel_id=1, source_target_pairs={{0,4},{4,8},{8,12},{12,16},{16,20},{20,24},{24,28},{1,5},{5,9},{9,... | collective-permute-start | bytes 98312 | tf_op jit(solution)/shard_map/ppermute | solution.py:22
  57.2 7.5 %collective-permute-start.17 = (f32[64,1,128]{0,1,2:T(1,128)S(1)}, f32[64,1,128]{0,1,2:T(1,128)S(1)}, u32[]{:S(2)}, u32[]{:S(2)}) collective-permute-start(f32[64,1,128]{0,1,2:T(1,128)S(1)} %get-tuple-element.115), channel_id=1, source_target_pairs={{4,0},{8,4},{12,8},{16,12},{20,16},{24,20},{28,24},{5,1},{9,5},{13... | collective-permute-start | bytes 98312 | tf_op jit(solution)/shard_map/ppermute | solution.py:23
  59.2 22.5 %collective-permute-start.26 = (f32[64,1,32]{0,2,1:T(8,128)S(1)}, f32[64,1,32]{0,2,1:T(8,128)S(1)}, u32[]{:S(2)}, u32[]{:S(2)}) collective-permute-start(f32[64,1,32]{0,2,1:T(8,128)S(1)} %get-tuple-element.138), channel_id=1, source_target_pairs={{0,4},{4,8},{8,12},{12,16},{16,20},{20,24},{24,28},{1,5},{5,9},{9,... | collective-permute-start | bytes 24584 | tf_op jit(solution)/shard_map/ppermute | solution.py:22
  62.8 18.8 %collective-permute-start.25 = (f32[64,1,32]{0,2,1:T(8,128)S(1)}, f32[64,1,32]{0,2,1:T(8,128)S(1)}, u32[]{:S(2)}, u32[]{:S(2)}) collective-permute-start(f32[64,1,32]{0,2,1:T(8,128)S(1)} %get-tuple-element.139), channel_id=1, source_target_pairs={{4,0},{8,4},{12,8},{16,12},{20,16},{24,20},{28,24},{5,1},{9,5},{13... | collective-permute-start | bytes 24584 | tf_op jit(solution)/shard_map/ppermute | solution.py:23
  64.8 5.9 %collective-permute-start.19 = (f32[64,34,1]{0,1,2:T(8,128)S(1)}, f32[64,34,1]{0,1,2:T(8,128)S(1)}, u32[]{:S(2)}, u32[]{:S(2)}) collective-permute-start(f32[64,34,1]{0,1,2:T(8,128)S(1)} %get-tuple-element.106), channel_id=1, source_target_pairs={{1,0},{2,1},{3,2},{5,4},{6,5},{7,6},{9,8},{10,9},{11,10},{13,12},{... | collective-permute-start | bytes 26120 | tf_op jit(solution)/shard_map/ppermute | solution.py:23
  75.2 12.3 %collective-permute-start.22 = (f32[64,1,128]{0,1,2:T(1,128)S(1)}, f32[64,1,128]{0,1,2:T(1,128)S(1)}, u32[]{:S(2)}, u32[]{:S(2)}) collective-permute-start(f32[64,1,128]{0,1,2:T(1,128)S(1)} %get-tuple-element.112), channel_id=1, source_target_pairs={{0,4},{4,8},{8,12},{12,16},{16,20},{20,24},{24,28},{1,5},{5,9},{9,... | collective-permute-start | bytes 98312 | tf_op jit(solution)/shard_map/ppermute | solution.py:22
  79.7 7.8 %collective-permute-start.21 = (f32[64,1,128]{0,1,2:T(1,128)S(1)}, f32[64,1,128]{0,1,2:T(1,128)S(1)}, u32[]{:S(2)}, u32[]{:S(2)}) collective-permute-start(f32[64,1,128]{0,1,2:T(1,128)S(1)} %get-tuple-element.113), channel_id=1, source_target_pairs={{4,0},{8,4},{12,8},{16,12},{20,16},{24,20},{28,24},{5,1},{9,5},{13... | collective-permute-start | bytes 98312 | tf_op jit(solution)/shard_map/ppermute | solution.py:23
  81.7 11.7 %collective-permute-start.27 = (f32[64,10,1]{0,2,1:T(1,128)S(1)}, f32[64,10,1]{0,2,1:T(1,128)S(1)}, u32[]{:S(2)}, u32[]{:S(2)}) collective-permute-start(f32[64,10,1]{0,2,1:T(1,128)S(1)} %get-tuple-element.132), channel_id=1, source_target_pairs={{1,0},{2,1},{3,2},{5,4},{6,5},{7,6},{9,8},{10,9},{11,10},{13,12},{... | collective-permute-start | bytes 7688 | tf_op jit(solution)/shard_map/ppermute | solution.py:23
  83.0 10.4 %collective-permute-start.28 = (f32[64,10,1]{0,2,1:T(1,128)S(1)}, f32[64,10,1]{0,2,1:T(1,128)S(1)}, u32[]{:S(2)}, u32[]{:S(2)}) collective-permute-start(f32[64,10,1]{0,2,1:T(1,128)S(1)} %get-tuple-element.133), channel_id=1, source_target_pairs={{0,1},{1,2},{2,3},{4,5},{5,6},{6,7},{8,9},{9,10},{10,11},{12,13},{... | collective-permute-start | bytes 7688 | tf_op jit(solution)/shard_map/ppermute | solution.py:22
  87.6 5.9 %collective-permute-start.23 = (f32[64,34,1]{0,1,2:T(8,128)S(1)}, f32[64,34,1]{0,1,2:T(8,128)S(1)}, u32[]{:S(2)}, u32[]{:S(2)}) collective-permute-start(f32[64,34,1]{0,1,2:T(8,128)S(1)} %get-tuple-element.104), channel_id=1, source_target_pairs={{1,0},{2,1},{3,2},{5,4},{6,5},{7,6},{9,8},{10,9},{11,10},{13,12},{... | collective-permute-start | bytes 26120 | tf_op jit(solution)/shard_map/ppermute | solution.py:23
  98.9 6.7 %collective-permute-start = (f32[64,1,32]{0,2,1:T(8,128)S(1)}, f32[64,1,32]{0,2,1:T(8,128)S(1)}, u32[]{:S(2)}, u32[]{:S(2)}) collective-permute-start(f32[64,1,32]{0,2,1:T(8,128)S(1)} %get-tuple-element.209), channel_id=1, source_target_pairs={{0,4},{4,8},{8,12},{12,16},{16,20},{20,24},{24,28},{1,5},{5,9},{9,... | collective-permute-start | bytes 24584 | tf_op jit(solution)/shard_map/while/body/eval_jaxpr/ppermute | solution.py:22
  117.5 5.6 %collective-permute-start.4 = (f32[64,1,32]{0,2,1:T(8,128)S(1)}, f32[64,1,32]{0,2,1:T(8,128)S(1)}, u32[]{:S(2)}, u32[]{:S(2)}) collective-permute-start(f32[64,1,32]{0,2,1:T(8,128)S(1)} %get-tuple-element.213), channel_id=1, source_target_pairs={{4,0},{8,4},{12,8},{16,12},{20,16},{24,20},{28,24},{5,1},{9,5},{13... | collective-permute-start | bytes 24584 | tf_op jit(solution)/shard_map/while/body/eval_jaxpr/ppermute | solution.py:23
  136.4 6.8 %collective-permute-start.8 = (f32[64,8,32]{0,2,1:T(8,128)S(1)}, f32[64,8,32]{0,2,1:T(8,128)S(1)}, u32[]{:S(2)}, u32[]{:S(2)}) collective-permute-start(f32[64,8,32]{0,2,1:T(8,128)S(1)} %broadcast_multiply_fusion.4), channel_id=1, source_target_pairs={{0,32},{32,64},{64,96},{96,128},{128,160},{160,192},{192,224},{1,3... | collective-permute-start | bytes 196616 | tf_op jit(solution)/shard_map/while/body/eval_jaxpr/ppermute | solution.py:31
  143.3 6.6 %collective-permute-start = (f32[64,1,32]{0,2,1:T(8,128)S(1)}, f32[64,1,32]{0,2,1:T(8,128)S(1)}, u32[]{:S(2)}, u32[]{:S(2)}) collective-permute-start(f32[64,1,32]{0,2,1:T(8,128)S(1)} %get-tuple-element.209), channel_id=1, source_target_pairs={{0,4},{4,8},{8,12},{12,16},{16,20},{20,24},{24,28},{1,5},{5,9},{9,... | collective-permute-start | bytes 24584 | tf_op jit(solution)/shard_map/while/body/eval_jaxpr/ppermute | solution.py:22
  180.3 7.0 %collective-permute-start.8 = (f32[64,8,32]{0,2,1:T(8,128)S(1)}, f32[64,8,32]{0,2,1:T(8,128)S(1)}, u32[]{:S(2)}, u32[]{:S(2)}) collective-permute-start(f32[64,8,32]{0,2,1:T(8,128)S(1)} %broadcast_multiply_fusion.4), channel_id=1, source_target_pairs={{0,32},{32,64},{64,96},{96,128},{128,160},{160,192},{192,224},{1,3... | collective-permute-start | bytes 196616 | tf_op jit(solution)/shard_map/while/body/eval_jaxpr/ppermute | solution.py:31
  187.4 7.1 %collective-permute-start = (f32[64,1,32]{0,2,1:T(8,128)S(1)}, f32[64,1,32]{0,2,1:T(8,128)S(1)}, u32[]{:S(2)}, u32[]{:S(2)}) collective-permute-start(f32[64,1,32]{0,2,1:T(8,128)S(1)} %get-tuple-element.209), channel_id=1, source_target_pairs={{0,4},{4,8},{8,12},{12,16},{16,20},{20,24},{24,28},{1,5},{5,9},{9,... | collective-permute-start | bytes 24584 | tf_op jit(solution)/shard_map/while/body/eval_jaxpr/ppermute | solution.py:22
  224.8 7.0 %collective-permute-start.8 = (f32[64,8,32]{0,2,1:T(8,128)S(1)}, f32[64,8,32]{0,2,1:T(8,128)S(1)}, u32[]{:S(2)}, u32[]{:S(2)}) collective-permute-start(f32[64,8,32]{0,2,1:T(8,128)S(1)} %broadcast_multiply_fusion.4), channel_id=1, source_target_pairs={{0,32},{32,64},{64,96},{96,128},{128,160},{160,192},{192,224},{1,3... | collective-permute-start | bytes 196616 | tf_op jit(solution)/shard_map/while/body/eval_jaxpr/ppermute | solution.py:31
  231.9 7.1 %collective-permute-start = (f32[64,1,32]{0,2,1:T(8,128)S(1)}, f32[64,1,32]{0,2,1:T(8,128)S(1)}, u32[]{:S(2)}, u32[]{:S(2)}) collective-permute-start(f32[64,1,32]{0,2,1:T(8,128)S(1)} %get-tuple-element.209), channel_id=1, source_target_pairs={{0,4},{4,8},{8,12},{12,16},{16,20},{20,24},{24,28},{1,5},{5,9},{9,... | collective-permute-start | bytes 24584 | tf_op jit(solution)/shard_map/while/body/eval_jaxpr/ppermute | solution.py:22
  269.2 7.0 %collective-permute-start.8 = (f32[64,8,32]{0,2,1:T(8,128)S(1)}, f32[64,8,32]{0,2,1:T(8,128)S(1)}, u32[]{:S(2)}, u32[]{:S(2)}) collective-permute-start(f32[64,8,32]{0,2,1:T(8,128)S(1)} %broadcast_multiply_fusion.4), channel_id=1, source_target_pairs={{0,32},{32,64},{64,96},{96,128},{128,160},{160,192},{192,224},{1,3... | collective-permute-start | bytes 196616 | tf_op jit(solution)/shard_map/while/body/eval_jaxpr/ppermute | solution.py:31
  276.3 7.1 %collective-permute-start = (f32[64,1,32]{0,2,1:T(8,128)S(1)}, f32[64,1,32]{0,2,1:T(8,128)S(1)}, u32[]{:S(2)}, u32[]{:S(2)}) collective-permute-start(f32[64,1,32]{0,2,1:T(8,128)S(1)} %get-tuple-element.209), channel_id=1, source_target_pairs={{0,4},{4,8},{8,12},{12,16},{16,20},{20,24},{24,28},{1,5},{5,9},{9,... | collective-permute-start | bytes 24584 | tf_op jit(solution)/shard_map/while/body/eval_jaxpr/ppermute | solution.py:22
  313.7 7.9 %collective-permute-start.8 = (f32[64,8,32]{0,2,1:T(8,128)S(1)}, f32[64,8,32]{0,2,1:T(8,128)S(1)}, u32[]{:S(2)}, u32[]{:S(2)}) collective-permute-start(f32[64,8,32]{0,2,1:T(8,128)S(1)} %broadcast_multiply_fusion.4), channel_id=1, source_target_pairs={{0,32},{32,64},{64,96},{96,128},{128,160},{160,192},{192,224},{1,3... | collective-permute-start | bytes 196616 | tf_op jit(solution)/shard_map/while/body/eval_jaxpr/ppermute | solution.py:31
  321.6 7.1 %collective-permute-start = (f32[64,1,32]{0,2,1:T(8,128)S(1)}, f32[64,1,32]{0,2,1:T(8,128)S(1)}, u32[]{:S(2)}, u32[]{:S(2)}) collective-permute-start(f32[64,1,32]{0,2,1:T(8,128)S(1)} %get-tuple-element.209), channel_id=1, source_target_pairs={{0,4},{4,8},{8,12},{12,16},{16,20},{20,24},{24,28},{1,5},{5,9},{9,... | collective-permute-start | bytes 24584 | tf_op jit(solution)/shard_map/while/body/eval_jaxpr/ppermute | solution.py:22
  358.9 8.2 %collective-permute-start.8 = (f32[64,8,32]{0,2,1:T(8,128)S(1)}, f32[64,8,32]{0,2,1:T(8,128)S(1)}, u32[]{:S(2)}, u32[]{:S(2)}) collective-permute-start(f32[64,8,32]{0,2,1:T(8,128)S(1)} %broadcast_multiply_fusion.4), channel_id=1, source_target_pairs={{0,32},{32,64},{64,96},{96,128},{128,160},{160,192},{192,224},{1,3... | collective-permute-start | bytes 196616 | tf_op jit(solution)/shard_map/while/body/eval_jaxpr/ppermute | solution.py:31
  367.2 7.1 %collective-permute-start = (f32[64,1,32]{0,2,1:T(8,128)S(1)}, f32[64,1,32]{0,2,1:T(8,128)S(1)}, u32[]{:S(2)}, u32[]{:S(2)}) collective-permute-start(f32[64,1,32]{0,2,1:T(8,128)S(1)} %get-tuple-element.209), channel_id=1, source_target_pairs={{0,4},{4,8},{8,12},{12,16},{16,20},{20,24},{24,28},{1,5},{5,9},{9,... | collective-permute-start | bytes 24584 | tf_op jit(solution)/shard_map/while/body/eval_jaxpr/ppermute | solution.py:22
  404.6 8.2 %collective-permute-start.8 = (f32[64,8,32]{0,2,1:T(8,128)S(1)}, f32[64,8,32]{0,2,1:T(8,128)S(1)}, u32[]{:S(2)}, u32[]{:S(2)}) collective-permute-start(f32[64,8,32]{0,2,1:T(8,128)S(1)} %broadcast_multiply_fusion.4), channel_id=1, source_target_pairs={{0,32},{32,64},{64,96},{96,128},{128,160},{160,192},{192,224},{1,3... | collective-permute-start | bytes 196616 | tf_op jit(solution)/shard_map/while/body/eval_jaxpr/ppermute | solution.py:31
  412.9 7.1 %collective-permute-start.30 = (f32[64,1,32]{0,2,1:T(8,128)S(1)}, f32[64,1,32]{0,2,1:T(8,128)S(1)}, u32[]{:S(2)}, u32[]{:S(2)}) collective-permute-start(f32[64,1,32]{0,2,1:T(8,128)S(1)} %get-tuple-element.137), channel_id=1, source_target_pairs={{0,4},{4,8},{8,12},{12,16},{16,20},{20,24},{24,28},{1,5},{5,9},{9,... | collective-permute-start | bytes 24584 | tf_op jit(solution)/shard_map/ppermute | solution.py:22
  423.1 5.8 %collective-permute-start.31 = (f32[64,10,1]{0,2,1:T(1,128)S(1)}, f32[64,10,1]{0,2,1:T(1,128)S(1)}, u32[]{:S(2)}, u32[]{:S(2)}) collective-permute-start(f32[64,10,1]{0,2,1:T(1,128)S(1)} %get-tuple-element.130), channel_id=1, source_target_pairs={{1,0},{2,1},{3,2},{5,4},{6,5},{7,6},{9,8},{10,9},{11,10},{13,12},{... | collective-permute-start | bytes 7688 | tf_op jit(solution)/shard_map/ppermute | solution.py:23
  (66 other events, 397.0 us)
where the time goes:
time: 463 us; the launch traced here: 455 us
  starting transfers between devices  274 us (59%)
  waiting for transfers between devices  92.4 us (20%)
  other arithmetic  57.5 us (12%)
  local copies, waits for them, and re-layouts  29.2 us (6%)
    ppermute x42, starting transfers between devices, extended(): before = lax.ppermute(last, axis, up)  175 us
    ppermute x42, starting transfers between devices, extended(): after = lax.ppermute(leading, axis, down)  67.7 us
    ppermute x42, waiting for transfers between devices, extended(): after = lax.ppermute(leading, axis, down)  56.5 us
    ppermute x7, starting transfers between devices, passed_along(): return lax.ppermute(block, axis, route)  31.3 us
    add x5, other arithmetic, advance(): return centre + time_step * (factor * diffuse * laplace - centre * slope)  24.1 us
    reduce_sum x8, other arithmetic, restrict(): return field.reshape(levels, rows // 4, 4, cols // 4, 4).mean(axis=(2, 4))  24 us
    ppermute x7, waiting for transfers between devices, passed_along(): return lax.ppermute(block, axis, route)  20.9 us
    another operation x29, local copies, waits for them, and re-layouts, prolong(): jnp.stack(parts, axis=3).reshape(levels, 4 * coarse_rows, 4 * coarse_cols)  15.3 us
  transfers between devices with their start and end apart: 91, of which 44 were waited for; matrix products, arithmetic and copies ran while one was open for 2% of the time, Pallas kernels for 0%

commit v1 on v0

v1 whole, which is shorter than its diff:
```python
import jax
import jax.numpy as jnp
from jax import lax
from jax.experimental import pallas as pl
from jax.experimental.pallas import tpu as pltpu
from jax.sharding import PartitionSpec as P

SUB = 4
STEP = 0.2
LEVELS = 64
NX = 32
HALF = 64
CX = NX // 4
CY = HALF // 4
W = 128
WEIGHTS_LOW = (0.375, 0.125, 0.0, 0.0)
WEIGHTS_MID = (0.625, 0.875, 0.875, 0.625)
WEIGHTS_HIGH = (0.0, 0.0, 0.125, 0.375)
BLEND = (0.125, 0.75, 0.125)
F32 = jnp.float32

STRIP = 4 * HALF + CY
SIDE = 20 * 8 + 8
FROWS = 88
CROWS = 40
OROWS = 24


def lanes(rows):
    return lax.broadcasted_iota(jnp.int32, (rows, W), 1)


def rows_of(rows):
    return lax.broadcasted_iota(jnp.int32, (rows, W), 0)


def low(rows):
    return lanes(rows) < LEVELS


def swap(value):
    return pltpu.roll(value, LEVELS, 1)


def coarse_rows(ref, start, count):
    total = ref[pl.ds(start, count, stride=4), :]
    for offset in range(1, 4):
        total = total + ref[pl.ds(start + offset, count, stride=4), :]
    return total * (1.0 / 16.0)


def pack_kernel(u_ref, t_ref, first_ref, last_ref, sum_ref):
    lo = low(HALF)
    for x in range(0, NX, 2):
        both = jnp.concatenate(
            [u_ref[pl.ds(x, LEVELS, stride=NX), :], u_ref[pl.ds(x + 1, LEVELS, stride=NX), :]], axis=0
        ).T
        top = both[:HALF]
        bottom = both[HALF:]
        t_ref[x * HALF : (x + 1) * HALF, :] = jnp.where(lo, top, swap(bottom))
        t_ref[(x + 1) * HALF : (x + 2) * HALF, :] = jnp.where(lo, swap(top), bottom)

    def row(x):
        return t_ref[x * HALF : (x + 1) * HALF, :]

    first_ref[: 4 * HALF, :] = t_ref[: 4 * HALF, :]
    sum_ref[...] = (row(4) + row(5)) + (row(6) + row(7))
    first_ref[4 * HALF :, :] = coarse_rows(sum_ref, 0, CY)
    last_ref[: 4 * HALF, :] = t_ref[(NX - 4) * HALF :, :]
    sum_ref[...] = (row(NX - 8) + row(NX - 7)) + (row(NX - 6) + row(NX - 5))
    last_ref[4 * HALF :, :] = coarse_rows(sum_ref, 0, CY)


def side_kernel(t_ref, west_ref, east_ref, left_ref, right_ref):
    lo = low(8)

    def edge(x, start):
        if x < 0:
            base = (x + 4) * HALF
            return west_ref[base + start : base + start + 8, :]
        if x >= NX:
            base = (x - NX) * HALF
            return east_ref[base + start : base + start + 8, :]
        return t_ref[x * HALF + start : x * HALF + start + 8, :]

    for i in range(20):
        left_ref[8 * i : 8 * i + 8, :] = jnp.where(lo, edge(i - 4, 0), swap(edge(i + 16, 0)))
        right_ref[8 * i : 8 * i + 8, :] = jnp.where(
            lo, swap(edge(i - 4, HALF - 8)), edge(i + 16, HALF - 8)
        )
    base = 4 * HALF
    left_ref[160:168, :] = jnp.where(lo, west_ref[base : base + 8, :], swap(east_ref[base : base + 8, :]))
    right_ref[160:168, :] = jnp.where(
        lo, swap(west_ref[base + 8 : base + 16, :]), east_ref[base + 8 : base + 16, :]
    )


def both_halves(values):
    return jnp.concatenate([values, values], axis=1)


def fine_kernel(
    place_ref, t_ref, west_ref, east_ref, left_ref, right_ref, diffuse_ref, wind_ref,
    end_ref, image_ref, send_ref,
    a_ref, b_ref, sum_ref, coarse_ref, change_ref, blend_ref, part_ref,
):
    first_segment = place_ref[0] == 0
    at_west = place_ref[1] == 0
    at_east = place_ref[1] == 7
    at_left = place_ref[2] == 0
    at_right = place_ref[2] == 3
    lo8 = low(8)
    zero8 = jnp.zeros((8, W), F32)

    for i in range(40):
        x = i - 4
        if x < 0:
            source, base, outside = west_ref, (x + 4) * HALF, at_west
        elif x >= NX:
            source, base, outside = east_ref, (x - NX) * HALF, at_east
        else:
            source, base, outside = t_ref, x * HALF, None
        rows = source[base : base + HALF, :]
        j = i % 20
        from_left = left_ref[8 * j : 8 * j + 8, :]
        from_right = right_ref[8 * j : 8 * j + 8, :]
        if i >= 20:
            from_left = swap(from_left)
        else:
            from_right = swap(from_right)
        from_left = jnp.where(at_left, zero8, from_left)
        from_right = jnp.where(at_right, zero8, from_right)
        before = jnp.where(lo8, from_left, swap(rows[HALF - 8 :]))
        after = jnp.where(lo8, swap(rows[:8]), from_right)
        if outside is not None:
            rows = jnp.where(outside, jnp.zeros_like(rows), rows)
            before = jnp.where(outside, zero8, before)
            after = jnp.where(outside, zero8, after)
        start = i * FROWS
        a_ref[start : start + 4, :] = zero8[:4]
        a_ref[start + 4 : start + 12, :] = before
        a_ref[start + 12 : start + 76, :] = rows
        a_ref[start + 76 : start + 84, :] = after
        a_ref[start + 84 : start + 88, :] = zero8[:4]

    diffuse = both_halves(diffuse_ref[...])
    wind = both_halves(wind_ref[...])
    spread = jnp.broadcast_to(STEP * diffuse, (8, W))
    along_x = jnp.broadcast_to((0.5 * STEP) * wind[0:1], (8, W))
    along_y = jnp.broadcast_to((0.5 * STEP) * wind[1:2], (8, W))

    def advanced(centre, east, west, north, south, kd):
        slope = along_x * (east - west) + along_y * (north - south)
        return centre + (kd * ((east + west) + (north + south) - 4.0 * centre) - centre * slope)

    coarse_ref[...] = jnp.zeros_like(coarse_ref)
    for j in range(10):
        base = 4 * j * FROWS
        sum_ref[...] = (a_ref[base : base + FROWS, :] + a_ref[base + FROWS : base + 2 * FROWS, :]) + (
            a_ref[base + 2 * FROWS : base + 3 * FROWS, :] + a_ref[base + 3 * FROWS : base + 4 * FROWS, :]
        )
        start = (j + 1) * CROWS
        coarse_ref[start + 7 : start + 27, :] = coarse_rows(sum_ref, 4, 20)
    left_corner = left_ref[160:168, :]
    right_corner = right_ref[160:168, :]
    for source, start, outside, is_west in (
        (west_ref, 0, at_west, True),
        (east_ref, 11 * CROWS, at_east, False),
    ):
        rows = source[4 * HALF :, :]
        from_left = left_corner if is_west else swap(left_corner)
        from_right = swap(right_corner) if is_west else right_corner
        from_left = jnp.where(at_left, zero8, from_left)
        from_right = jnp.where(at_right, zero8, from_right)
        before = jnp.where(lo8, from_left, swap(rows[8:]))
        after = jnp.where(lo8, swap(rows[:8]), from_right)
        coarse_ref[start + 1 : start + 9, :] = jnp.where(outside, zero8, before)
        coarse_ref[start + 9 : start + 25, :] = jnp.where(outside, jnp.zeros_like(rows), rows)
        coarse_ref[start + 25 : start + 33, :] = jnp.where(outside, zero8, after)

    for j in range(10):
        for tile in range(3):
            r = (j + 1) * CROWS + 8 + 8 * tile
            image = advanced(
                coarse_ref[r : r + 8, :],
                coarse_ref[r + CROWS : r + CROWS + 8, :],
                coarse_ref[r - CROWS : r - CROWS + 8, :],
                coarse_ref[r + 1 : r + 9, :],
                coarse_ref[r - 1 : r + 7, :],
                0.25 * spread,
            )
            cy = rows_of(8) + (8 * tile - 1)
            outside = cy > CY
            if tile == 0:
                outside = jnp.logical_or(outside, jnp.logical_and(at_left, jnp.logical_and(cy < 0, lo8)))
            if tile == 2:
                outside = jnp.logical_or(
                    outside, jnp.logical_and(at_right, jnp.logical_and(cy >= CY, jnp.logical_not(lo8)))
                )
            if j == 0:
                outside = jnp.logical_or(outside, at_west)
            if j == 9:
                outside = jnp.logical_or(outside, at_east)
            image = jnp.where(outside, zero8, image)
            o = j * OROWS + 8 * tile
            image_ref[o : o + 8, :] = image
            change_ref[o : o + 8, :] = jnp.where(first_segment, image, zero8) - image

    left_out = jnp.logical_and(at_left, jnp.logical_and(rows_of(8) < 4, lo8))
    right_out = jnp.logical_and(at_right, jnp.logical_and(rows_of(8) >= 4, jnp.logical_not(lo8)))
    buffers = (a_ref, b_ref)
    for step in range(SUB):
        source = buffers[step % 2]
        target = buffers[(step + 1) % 2]
        last = step == SUB - 1
        begin = step + 1
        stop = 40 - begin
        if not last:
            for tile in range(9):

                def row_step(i, tile=tile, source=source, target=target):
                    r = i * FROWS + 8 + 8 * tile
                    value = advanced(
                        source[pl.ds(r, 8), :],
                        source[pl.ds(r + FROWS, 8), :],
                        source[pl.ds(r - FROWS, 8), :],
                        source[pl.ds(r + 1, 8), :],
                        source[pl.ds(r - 1, 8), :],
                        spread,
                    )
                    if tile == 0:
                        value = jnp.where(left_out, zero8, value)
                    if tile == 8:
                        value = jnp.where(right_out, zero8, value)
                    return r, value

                for i in range(begin, stop):
                    r, value = row_step(i)
                    if i < 4:
                        value = jnp.where(at_west, zero8, value)
                    if i >= 36:
                        value = jnp.where(at_east, zero8, value)
                    target[pl.ds(r, 8), :] = value
        else:
            for tile in range(8):
                for i in range(begin, stop):
                    r = i * FROWS + 12 + 8 * tile
                    value = advanced(
                        source[r : r + 8, :],
                        source[r + FROWS : r + FROWS + 8, :],
                        source[r - FROWS : r - FROWS + 8, :],
                        source[r + 1 : r + 9, :],
                        source[r - 1 : r + 7, :],
                        spread,
                    )
                    o = (i - 4) * HALF + 8 * tile
                    end_ref[o : o + 8, :] = value

    for j in range(CX):
        lower = change_ref[j * OROWS : (j + 1) * OROWS, :]
        middle = change_ref[(j + 1) * OROWS : (j + 2) * OROWS, :]
        upper = change_ref[(j + 2) * OROWS : (j + 3) * OROWS, :]
        blend_ref[...] = BLEND[0] * lower + BLEND[1] * middle + BLEND[2] * upper
        blended = (
            BLEND[0] * blend_ref[0:CY, :] + BLEND[1] * blend_ref[1 : CY + 1, :] + BLEND[2] * blend_ref[2 : CY + 2, :]
        )
        base = 4 * j * HALF
        sum_ref[0:HALF, :] = (end_ref[base : base + HALF, :] + end_ref[base + HALF : base + 2 * HALF, :]) + (
            end_ref[base + 2 * HALF : base + 3 * HALF, :] + end_ref[base + 3 * HALF : base + 4 * HALF, :]
        )
        part_ref[j * CY : (j + 1) * CY, :] = coarse_rows(sum_ref, 0, CY) + blended
    turned = part_ref[...].T
    for g in range(4):
        for h in range(2):
            send_ref[pl.ds(2 * g + h, LEVELS, stride=8), :] = turned[h * LEVELS : (h + 1) * LEVELS]


def chain_kernel(place_ref, diffuse_ref, wind_ref, part_ref, send_ref, pad_ref):
    level = place_ref[0] * 8 + place_ref[1]
    gy = place_ref[2]
    spread = (0.25 * STEP) * diffuse_ref[level]
    along_x = (0.5 * STEP) * wind_ref[0, level]
    along_y = (0.5 * STEP) * wind_ref[1, level]

    lane = lanes(64)
    row = rows_of(64)
    block = row % 8
    column = lane % 16
    zero = jnp.zeros((64, W), F32)

    def shifted(value):
        turned = pltpu.roll(value, W - 16, 1)
        following = jnp.where(row < 56, pltpu.roll(turned, 56, 0), zero)
        east = jnp.where(lane < W - 16, turned, following)
        turned = pltpu.roll(value, 16, 1)
        previous = jnp.where(row >= 8, pltpu.roll(turned, 8, 0), zero)
        west = jnp.where(lane >= 16, turned, previous)
        return east, west

    def shifted_y(value):
        following = jnp.where(block < 7, pltpu.roll(value, 63, 0), zero)
        north = jnp.where(column < 15, pltpu.roll(value, W - 1, 1), pltpu.roll(following, 15, 1))
        previous = jnp.where(block > 0, pltpu.roll(value, 1, 0), zero)
        south = jnp.where(column > 0, pltpu.roll(value, 1, 1), pltpu.roll(previous, W - 15, 1))
        return north, south

    pad_ref[...] = jnp.zeros_like(pad_ref)
    for r in range(3):
        send_ref[pl.ds(r, 8, stride=3), :] = jnp.zeros((8, W), F32)

    lane8 = lanes(8)
    item = lane8 % 64
    west_east = jnp.where(item < 16, item + 112, item - 16)
    west_east = jnp.where(item < 32, west_east, 0)
    left_column = item - 33
    right_column = item - 49
    side = jnp.where(item < 48, left_column * 16 + 15, right_column * 16)
    side = jnp.clip(side, 0, W - 1)

    coarse = part_ref[0:64, :]
    for n in range(1, 8):
        east, west = shifted(coarse)
        north, south = shifted_y(coarse)
        slope = along_x * (east - west) + along_y * (north - south)
        image = coarse + (spread * ((east + west) + (north + south) - 4.0 * coarse) - coarse * slope)
        for g in range(8):
            start = (g + 1) * 24 + 8
            pad_ref[start : start + 8, :] = image[8 * g : 8 * g + 8]

        def tiles(dx, b):
            return pad_ref[pl.ds((1 + dx) * 24 + 8 + b, 8, stride=24), :]

        b = 2 * gy
        rows = []
        for h in range(2):
            ends = jnp.where(lane8 >= 64, tiles(-1, b + h), tiles(1, b + h))
            ends = jnp.take_along_axis(ends, west_east, axis=1)
            sides = []
            for away in (-1, 1):
                own = jnp.take_along_axis(tiles(0, b + h + away), side, axis=1)
                at = 15 if away < 0 else 0
                lower = jnp.take_along_axis(tiles(-1, b + h + away), jnp.full((8, W), 112 + at, jnp.int32), axis=1)
                upper = jnp.take_along_axis(tiles(1, b + h + away), jnp.full((8, W), at, jnp.int32), axis=1)
                first = 32 if away < 0 else 48
                value = jnp.where(item == first, lower, jnp.where(item == first + 9, upper, own))
                sides.append(value)
            rows.append(jnp.where(item < 32, ends, jnp.where(item < 48, sides[0], sides[1])))
        base = n * 24
        send_ref[pl.ds(base, 8, stride=3), :] = tiles(0, b)
        send_ref[pl.ds(base + 1, 8, stride=3), :] = tiles(0, b + 1)
        send_ref[pl.ds(base + 2, 8, stride=3), :] = jnp.where(lane8 < 64, rows[0], rows[1])

        if n < 7:
            east, west = shifted(image)
            blended = BLEND[0] * west + BLEND[1] * image + BLEND[2] * east
            north, south = shifted_y(blended)
            blended = BLEND[0] * south + BLEND[1] * blended + BLEND[2] * north
            coarse = part_ref[n * 64 : (n + 1) * 64, :] + blended


def end_kernel(place_ref, end_ref, image_ref, back_ref, out_ref, change_ref, along_ref, fine_ref, turn_ref):
    first_segment = place_ref[0] == 0
    lo8 = low(8)
    main = jnp.concatenate(
        [back_ref[pl.ds(0, LEVELS, stride=3), :], back_ref[pl.ds(1, LEVELS, stride=3), :]], axis=0
    ).T
    ring = back_ref[pl.ds(2, LEVELS, stride=3), :]
    ring = jnp.concatenate([ring, ring], axis=0).T
    ring = jnp.where(low(64), ring[:64], ring[64:])

    change_ref[...] = jnp.zeros_like(change_ref)
    for j in range(10):
        start = j * OROWS
        if j == 0:
            rows = ring[0:16]
        elif j == 9:
            rows = ring[16:32]
        else:
            rows = main[(j - 1) * CY : j * CY]
        change_ref[start + 1 : start + 17, :] = rows
        change_ref[start : start + 1, :] = ring[32 + j : 33 + j]
        change_ref[start + 17 : start + 18, :] = ring[48 + j : 49 + j]
    for tile in range(10 * OROWS // 8):
        part = slice(8 * tile, 8 * tile + 8)
        image = image_ref[part, :]
        change_ref[part, :] = jnp.where(first_segment, image, change_ref[part, :]) - image

    lo = low(HALF)
    for j in range(CX):
        lower = change_ref[j * OROWS : (j + 1) * OROWS, :]
        middle = change_ref[(j + 1) * OROWS : (j + 2) * OROWS, :]
        upper = change_ref[(j + 2) * OROWS : (j + 3) * OROWS, :]
        for offset in range(4):
            along = WEIGHTS_MID[offset] * middle
            if offset < 2:
                along = along + WEIGHTS_LOW[offset] * lower
            else:
                along = along + WEIGHTS_HIGH[offset] * upper
            slot = offset * OROWS
            along_ref[slot : slot + OROWS, :] = along
            before = along_ref[slot : slot + CY, :]
            centre = along_ref[slot + 1 : slot + CY + 1, :]
            after = along_ref[slot + 2 : slot + CY + 2, :]
            for k in range(4):
                value = WEIGHTS_MID[k] * centre
                if k < 2:
                    value = value + WEIGHTS_LOW[k] * before
                else:
                    value = value + WEIGHTS_HIGH[k] * after
                fine_ref[pl.ds(offset * HALF + k, CY, stride=4), :] = value
        for pair in range(2):
            x = 4 * j + 2 * pair
            one = end_ref[x * HALF : (x + 1) * HALF, :] + fine_ref[2 * pair * HALF : (2 * pair + 1) * HALF, :]
            two = (
                end_ref[(x + 1) * HALF : (x + 2) * HALF, :]
                + fine_ref[(2 * pair + 1) * HALF : (2 * pair + 2) * HALF, :]
            )
            both = jnp.concatenate([jnp.where(lo, one, swap(two)), jnp.where(lo, swap(one), two)], axis=0).T
            out_ref[pl.ds(x, LEVELS, stride=NX), :] = both[:LEVELS]
            out_ref[pl.ds(x + 1, LEVELS, stride=NX), :] = both[LEVELS:]


def shape(rows):
    return jax.ShapeDtypeStruct((rows, W), F32)


VMEM = pl.BlockSpec(memory_space=pltpu.VMEM)
SMEM = pl.BlockSpec(memory_space=pltpu.SMEM)


def scratch(rows):
    return pltpu.VMEM((rows, W), F32)


def call(kernel, out_shape, in_specs, scratch_shapes, name):
    many = isinstance(out_shape, tuple)
    return pl.pallas_call(
        kernel,
        out_shape=out_shape,
        in_specs=in_specs,
        out_specs=(VMEM,) * len(out_shape) if many else VMEM,
        scratch_shapes=scratch_shapes,
        compiler_params=pltpu.CompilerParams(vmem_limit_bytes=24 * 1024 * 1024),
        name=name,
    )


def ring(array, axis, distance):
    devices = lax.axis_size(axis)
    return lax.ppermute(array, axis, [(i, (i + distance) % devices) for i in range(devices)])


def shards(state_starts, diffusivity, wind):
    place = jnp.stack([lax.axis_index(axis) for axis in ("tm", "gx", "gy")]).astype(jnp.int32)
    field = state_starts.reshape(LEVELS * NX, W)
    turned, first_rows, last_rows = call(
        pack_kernel, (shape(NX * HALF), shape(STRIP), shape(STRIP)), [VMEM], [scratch(HALF)], "pack"
    )(field)
    west = ring(last_rows, "gx", 1)
    east = ring(first_rows, "gx", -1)
    first_columns, last_columns = call(side_kernel, (shape(SIDE), shape(SIDE)), [VMEM] * 3, [], "sides")(
        turned, west, east
    )
    left = ring(last_columns, "gy", 1)
    right = ring(first_columns, "gy", -1)
    fine_end, image, parts = call(
        fine_kernel,
        (shape(NX * HALF), shape(10 * OROWS), shape(8 * LEVELS)),
        [SMEM] + [VMEM] * 7,
        [
            scratch(40 * FROWS), scratch(40 * FROWS), scratch(FROWS), scratch(12 * CROWS),
            scratch(10 * OROWS), scratch(OROWS), scratch(W),
        ],
        "fine",
    )(place, turned, west, east, left, right, diffusivity.reshape(1, LEVELS), wind)
    parts = lax.all_to_all(parts.reshape(256, 2, W), ("tm", "gx", "gy"), 0, 0, tiled=True)
    images = call(chain_kernel, shape(3 * 64), [SMEM, SMEM, SMEM, VMEM], [scratch(10 * 24)], "chain")(
        place, diffusivity, wind, parts.reshape(512, W)
    )
    images = lax.all_to_all(images.reshape(64, 3, W), ("tm", "gx"), 0, 0, tiled=True)
    ending = call(
        end_kernel,
        shape(LEVELS * NX),
        [SMEM] + [VMEM] * 3,
        [scratch(10 * OROWS), scratch(4 * OROWS), scratch(4 * HALF), scratch(HALF)],
        "ending",
    )(place, fine_end, image, images.reshape(192, W))
    return ending.reshape(1, LEVELS, NX, W)


def solution(mesh):
    placed = (P("tm", None, "gx", "gy"), P(), P())
    return jax.shard_map(
        shards, mesh=mesh, in_specs=placed, out_specs=P("tm", None, "gx", "gy"), check_vma=False
    )
```

time: 463 us -> 69.1 us (0.15); the launches traced: 455 us -> 68.9 us
  starting transfers between devices: 274 us -> 6.03 us
  waiting for transfers between devices: 92.4 us -> 5.9 us
  other arithmetic: 57.5 us -> 0.08 us
  blocking collectives: 0 us -> 45.5 us
  local copies, waits for them, and re-layouts: 29.2 us -> 1.32 us
  Pallas kernels: 0 us -> 10 us
    ppermute x91 -> x4, starting transfers between devices: 274 us -> 6.03 us  [ring(): lax.ppermute(array, axis, [(i, (i + distance) % devices) for i in range(d...]
    ppermute x91 -> x4, waiting for transfers between devices: 92.4 us -> 5.9 us  [ring(): lax.ppermute(array, axis, [(i, (i + distance) % devices) for i in range(d...]
    all_to_all x0 -> x2, blocking collectives: none -> 45.5 us  [the longest x1 29.9 us: shards(): lax.all_to_all(parts.reshape(256, 2, W), ('tm', 'gx', 'gy'), 0, 0, tiled=...]
    add x13 -> x0, other arithmetic: 30.1 us -> none  [the longest x5 24.1 us: advance(): return centre + time_step * (factor * diffuse * laplace - centre * slope)]
    reduce_sum x8 -> x0, other arithmetic: 24 us -> none  [restrict(): return field.reshape(levels, rows // 4, 4, cols // 4, 4).mean(axis=(2, 4))]
    another operation x38 -> x0, local copies, waits for them, and re-layouts: 18.2 us -> none  [the longest x29 15.3 us: prolong(): jnp.stack(parts, axis=3).reshape(levels, 4 * coarse_rows, 4 * coarse_cols)]
    pallas_call x0 -> x5, Pallas kernels: none -> 10 us  [the longest x1 3.41 us: shards(): call(fine_kernel, (shape(NX * HALF), shape(10 * OROWS), shape(8 * LEVELS)...]
    unnamed x18 -> x6, local copies, waits for them, and re-layouts: 6.57 us -> 1.23 us
  transfers between devices with their start and end apart: 91 -> 4, of which waited for: 44 -> 3; matrix products, arithmetic and copies ran while one was open for 2% -> 0% of each run, Pallas kernels for 0% -> 0%
where the time goes in v1:
time: 69.1 us; the launch traced here: 68.9 us
  blocking collectives  45.5 us (66%)
  Pallas kernels  10 us (14%)
  starting transfers between devices  6.03 us (9%)
  waiting for transfers between devices  5.9 us (9%)
  local copies, waits for them, and re-layouts  1.32 us (2%)
    all_to_all x1, blocking collectives, shards(): lax.all_to_all(parts.reshape(256, 2, W), ('tm', 'gx', 'gy'), 0, 0, tiled=...  29.9 us
    all_to_all x1, blocking collectives, shards(): lax.all_to_all(images.reshape(64, 3, W), ('tm', 'gx'), 0, 0, tiled=True)  15.6 us
    ppermute x4, starting transfers between devices, ring(): lax.ppermute(array, axis, [(i, (i + distance) % devices) for i in range(d...  6.03 us
    ppermute x4, waiting for transfers between devices, ring(): lax.ppermute(array, axis, [(i, (i + distance) % devices) for i in range(d...  5.9 us
    pallas_call x1, Pallas kernels, shards(): call(fine_kernel, (shape(NX * HALF), shape(10 * OROWS), shape(8 * LEVELS)...  3.41 us
    pallas_call x1, Pallas kernels, shards(): call(end_kernel, shape(LEVELS * NX), [SMEM] + [VMEM] * 3, [scratch(10 * O...  2.93 us
    pallas_call x1, Pallas kernels, shards(): call(chain_kernel, shape(3 * 64), [SMEM, SMEM, SMEM, VMEM], [scratch(10 *...  2.58 us
  transfers between devices with their start and end apart: 4, of which 3 were waited for; matrix products, arithmetic and copies ran while one was open for 0% of the time, Pallas kernels for 0%

profile of v1, /device:TPU:1, one launch (start us, length us, event | category | flops | bytes accessed | tf_op | source)
XLA Modules:
  0.0 68.9 jit_solution(12057201300742879590)
XLA Ops:
  0.0 0.0 copy-start
  0.0 1.2 %copy-done = f32[1,64,32,128]{3,2,1,0:T(8,128)S(1)} copy-done((f32[1,64,32,128]{3,2,1,0:T(8,128)S(1)}, f32[1,64,32,128]{3,2,1,0:T(8,128)}, u32[]{:S(2)}) %copy-start) | copy-done | bytes 1048600
  1.2 1.0 %pack.1 = (f32[2048,128]{1,0:T(8,128)S(1)}, f32[272,128]{1,0:T(8,128)S(1)}, f32[272,128]{1,0:T(8,128)S(1)}) custom-call(f32[2048,128]{1,0:T(8,128)S(1)} %bitcast.8), custom_call_target="tpu_custom_call" | custom-call | tf_op jit(solution)/shard_map/pack/pallas_call | solution.py:456
  2.2 2.6 %collective-permute-start = (f32[272,128]{1,0:T(8,128)S(1)}, f32[272,128]{1,0:T(8,128)S(1)}, u32[]{:S(2)}, u32[]{:S(2)}) collective-permute-start(f32[272,128]{1,0:T(8,128)S(1)} %get-tuple-element.14), channel_id=1, source_target_pairs={{0,4},{4,8},{8,12},{12,16},{16,20},{20,24},{24,28},{28,0},{1,5},{5... | collective-permute-start | bytes 417800 | tf_op jit(solution)/shard_map/ppermute | solution.py:450
  4.8 0.7 collective-permute-start.1
  5.5 1.4 %collective-permute-done.west_ref = f32[272,128]{1,0:T(8,128)S(1)} collective-permute-done((f32[272,128]{1,0:T(8,128)S(1)}, f32[272,128]{1,0:T(8,128)S(1)}, u32[]{:S(2)}, u32[]{:S(2)}) %collective-permute-start) | collective-permute-done | bytes 139296 | tf_op jit(solution)/shard_map/ppermute | solution.py:450
  6.8 2.8 %collective-permute-done.1.east_ref = f32[272,128]{1,0:T(8,128)S(1)} collective-permute-done((f32[272,128]{1,0:T(8,128)S(1)}, f32[272,128]{1,0:T(8,128)S(1)}, u32[]{:S(2)}, u32[]{:S(2)}) %collective-permute-start.1) | collective-permute-done | bytes 139296 | tf_op jit(solution)/shard_map/ppermute | solution.py:450
  9.6 0.1 sides.1
  9.7 1.1 %collective-permute-start.2 = (f32[168,128]{1,0:T(8,128)S(1)}, f32[168,128]{1,0:T(8,128)S(1)}, u32[]{:S(2)}, u32[]{:S(2)}) collective-permute-start(f32[168,128]{1,0:T(8,128)S(1)} %get-tuple-element.16), channel_id=1, source_target_pairs={{0,1},{1,2},{2,3},{3,0},{4,5},{5,6},{6,7},{7,4},{8,9},{9,10},{10,1... | collective-permute-start | bytes 258056 | tf_op jit(solution)/shard_map/ppermute | solution.py:450
  10.8 1.7 %collective-permute-start.3 = (f32[168,128]{1,0:T(8,128)S(1)}, f32[168,128]{1,0:T(8,128)S(1)}, u32[]{:S(2)}, u32[]{:S(2)}) collective-permute-start(f32[168,128]{1,0:T(8,128)S(1)} %get-tuple-element.17), channel_id=1, source_target_pairs={{0,3},{1,0},{2,1},{3,2},{4,7},{5,4},{6,5},{7,6},{8,11},{9,8},{10,9... | collective-permute-start | bytes 258056 | tf_op jit(solution)/shard_map/ppermute | solution.py:450
  12.5 0.1 pad_add_fusion.place_ref
  12.5 0.0 copy-start.1
  12.5 0.0 copy-start.2
  12.5 1.8 %collective-permute-done.2.left_ref = f32[168,128]{1,0:T(8,128)S(1)} collective-permute-done((f32[168,128]{1,0:T(8,128)S(1)}, f32[168,128]{1,0:T(8,128)S(1)}, u32[]{:S(2)}, u32[]{:S(2)}) %collective-permute-start.2) | collective-permute-done | bytes 86048 | tf_op jit(solution)/shard_map/ppermute | solution.py:450
  14.3 0.0 collective-permute-done.3.right_ref
  14.3 0.0 copy-done.1
  14.3 0.0 copy-done.2
  14.3 3.4 %fine.1 = (f32[2048,128]{1,0:T(8,128)S(1)}, f32[240,128]{1,0:T(8,128)S(1)}, f32[512,128]{1,0:T(8,128)S(1)}) custom-call(s32[3]{0:T(128)S(1)} %pad_add_fusion.place_ref, f32[2048,128]{1,0:T(8,128)S(1)} %get-tuple-element.13.t_ref, f32[272,128]{1,0:T(8,128)S(1)} %collective-permute-done.west_ref, f32[272,128]{1,0:T(8,128)S(1)} %collective-permute-done.1.east_ref, ...), custom_call_target="tpu_custom_call" | custom-call | tf_op jit(solution)/shard_map/fine/pallas_call | solution.py:466
  17.8 29.9 %all_to_all.10 = f32[256,2,128]{2,1,0:T(2,128)S(1)} all-to-all(f32[256,2,128]{2,1,0:T(2,128)S(1)} %bitcast.10), channel_id=1, replica_groups=mesh['tm'=8,'gx'=8,'gy'=4] {'tm','gx','gy'}, dimensions={0} | all-to-all | bytes 524288 | tf_op jit(solution)/shard_map/all_to_all | solution.py:476
  47.7 2.6 %chain.1 = f32[192,128]{1,0:T(8,128)S(1)} custom-call(s32[3]{0:T(128)S(1)} %pad_add_fusion.place_ref, f32[64]{0:T(128)S(1)} %copy-done.2, f32[2,64]{1,0:T(2,128)S(1)} %copy-done.1, f32[512,128]{1,0:T(8,128)S(1)} %bitcast.9), custom_call_target="tpu_custom_call" | custom-call | tf_op jit(solution)/shard_map/chain/pallas_call | solution.py:477
  50.3 15.6 %all_to_all.11 = f32[64,3,128]{2,1,0:T(4,128)S(1)} all-to-all(f32[64,3,128]{2,1,0:T(4,128)S(1)} %reshape.25), channel_id=1, replica_groups=mesh['tm'=8,'gx'=8,'gy'=4] {'tm','gx'}, dimensions={0} | all-to-all | bytes 196608 | tf_op jit(solution)/shard_map/all_to_all | solution.py:480
  66.0 2.9 %ending.1 = f32[2048,128]{1,0:T(8,128)} custom-call(s32[3]{0:T(128)S(1)} %pad_add_fusion.place_ref, f32[2048,128]{1,0:T(8,128)S(1)} %get-tuple-element.18.end_ref, f32[240,128]{1,0:T(8,128)S(1)} %get-tuple-element.19.image_ref, f32[192,128]{1,0:T(8,128)S(1)} %reshape.26.back_ref), custom_call_target="tpu_custom_call" | custom-call | tf_op jit(solution)/shard_map/ending/pallas_call | solution.py:481
  (2 shorter events, 0.1 us)
Async XLA Ops:
  0.0 1.2 %copy-start = (f32[1,64,32,128]{3,2,1,0:T(8,128)S(1)}, f32[1,64,32,128]{3,2,1,0:T(8,128)}, u32[]{:S(2)}) copy-start(f32[1,64,32,128]{3,2,1,0:T(8,128)} %param.3) | copy-start | bytes 3145732
  2.2 4.6 %collective-permute-start = (f32[272,128]{1,0:T(8,128)S(1)}, f32[272,128]{1,0:T(8,128)S(1)}, u32[]{:S(2)}, u32[]{:S(2)}) collective-permute-start(f32[272,128]{1,0:T(8,128)S(1)} %get-tuple-element.14), channel_id=1, source_target_pairs={{0,4},{4,8},{8,12},{12,16},{16,20},{20,24},{24,28},{28,0},{1,5},{5... | collective-permute-start | bytes 417800 | tf_op jit(solution)/shard_map/ppermute | solution.py:450
  4.8 4.8 %collective-permute-start.1 = (f32[272,128]{1,0:T(8,128)S(1)}, f32[272,128]{1,0:T(8,128)S(1)}, u32[]{:S(2)}, u32[]{:S(2)}) collective-permute-start(f32[272,128]{1,0:T(8,128)S(1)} %get-tuple-element.15), channel_id=1, source_target_pairs={{0,28},{4,0},{8,4},{12,8},{16,12},{20,16},{24,20},{28,24},{1,29},{... | collective-permute-start | bytes 417800 | tf_op jit(solution)/shard_map/ppermute | solution.py:450
  9.7 4.6 %collective-permute-start.2 = (f32[168,128]{1,0:T(8,128)S(1)}, f32[168,128]{1,0:T(8,128)S(1)}, u32[]{:S(2)}, u32[]{:S(2)}) collective-permute-start(f32[168,128]{1,0:T(8,128)S(1)} %get-tuple-element.16), channel_id=1, source_target_pairs={{0,1},{1,2},{2,3},{3,0},{4,5},{5,6},{6,7},{7,4},{8,9},{9,10},{10,1... | collective-permute-start | bytes 258056 | tf_op jit(solution)/shard_map/ppermute | solution.py:450
  10.8 3.5 %collective-permute-start.3 = (f32[168,128]{1,0:T(8,128)S(1)}, f32[168,128]{1,0:T(8,128)S(1)}, u32[]{:S(2)}, u32[]{:S(2)}) collective-permute-start(f32[168,128]{1,0:T(8,128)S(1)} %get-tuple-element.17), channel_id=1, source_target_pairs={{0,3},{1,0},{2,1},{3,2},{4,7},{5,4},{6,5},{7,6},{8,11},{9,8},{10,9... | collective-permute-start | bytes 258056 | tf_op jit(solution)/shard_map/ppermute | solution.py:450
  12.5 1.8 %copy-start.1 = (f32[2,64]{1,0:T(2,128)S(1)}, f32[2,64]{1,0:T(2,128)}, u32[]{:S(2)}) copy-start(f32[2,64]{1,0:T(2,128)} %wind_ref.3) | copy-start | bytes 1540
  12.5 1.8 %copy-start.2 = (f32[64]{0:T(128)S(1)}, f32[64]{0:T(128)}, u32[]{:S(2)}) copy-start(f32[64]{0:T(128)} %diffuse_ref.1) | copy-start | bytes 772

commit v2 on v1

--- a/solution.py
+++ b/solution.py
@@ -270,92 +270,111 @@
         )
         part_ref[j * CY : (j + 1) * CY, :] = coarse_rows(sum_ref, 0, CY) + blended
     turned = part_ref[...].T
-    for g in range(4):
-        for h in range(2):
-            send_ref[pl.ds(2 * g + h, LEVELS, stride=8), :] = turned[h * LEVELS : (h + 1) * LEVELS]
-
-
-def chain_kernel(place_ref, diffuse_ref, wind_ref, part_ref, send_ref, pad_ref):
+    for h in range(2):
+        send_ref[pl.ds(h, LEVELS, stride=2), :] = turned[h * LEVELS : (h + 1) * LEVELS]
+
+
+def split_kernel(part_ref, first_ref, second_ref):
+    first_ref[...] = part_ref[pl.ds(0, LEVELS, stride=2), :]
+    second_ref[...] = part_ref[pl.ds(1, LEVELS, stride=2), :]
+
+
+def chain_kernel(place_ref, diffuse_ref, wind_ref, part_ref, left_ref, right_ref, send_ref):
     level = place_ref[0] * 8 + place_ref[1]
-    gy = place_ref[2]
+    at_left = place_ref[2] == 0
+    at_right = place_ref[2] == 3
     spread = (0.25 * STEP) * diffuse_ref[level]
     along_x = (0.5 * STEP) * wind_ref[0, level]
     along_y = (0.5 * STEP) * wind_ref[1, level]
 
-    lane = lanes(64)
-    row = rows_of(64)
-    block = row % 8
+    lane = lanes(8)
+    row = rows_of(8)
     column = lane % 16
-    zero = jnp.zeros((64, W), F32)
-
-    def shifted(value):
-        turned = pltpu.roll(value, W - 16, 1)
-        following = jnp.where(row < 56, pltpu.roll(turned, 56, 0), zero)
-        east = jnp.where(lane < W - 16, turned, following)
-        turned = pltpu.roll(value, 16, 1)
-        previous = jnp.where(row >= 8, pltpu.roll(turned, 8, 0), zero)
-        west = jnp.where(lane >= 16, turned, previous)
+    zero = jnp.zeros((8, W), F32)
+
+    def neighbours(tile):
+        up = jnp.where(row < 7, pltpu.roll(tile, 7, 0), zero)
+        down = jnp.where(row > 0, pltpu.roll(tile, 1, 0), zero)
+        return up, down
+
+    def along_rows(tile, up, down):
+        east = pltpu.roll(jnp.where(lane < 16, up, tile), W - 16, 1)
+        west = pltpu.roll(jnp.where(lane >= W - 16, down, tile), 16, 1)
         return east, west
 
-    def shifted_y(value):
-        following = jnp.where(block < 7, pltpu.roll(value, 63, 0), zero)
-        north = jnp.where(column < 15, pltpu.roll(value, W - 1, 1), pltpu.roll(following, 15, 1))
-        previous = jnp.where(block > 0, pltpu.roll(value, 1, 0), zero)
-        south = jnp.where(column > 0, pltpu.roll(value, 1, 1), pltpu.roll(previous, W - 15, 1))
+    def along_columns(tiles):
+        after = [pltpu.roll(tile, W - 1, 1) for tile in tiles]
+        before = [pltpu.roll(tile, 1, 1) for tile in tiles]
+        after_far = [pltpu.roll(tile, 15, 1) for tile in tiles[1:]] + [zero]
+        before_far = [zero] + [pltpu.roll(tile, W - 15, 1) for tile in tiles[:-1]]
+        north = [jnp.where(column < 15, near, far) for near, far in zip(after, after_far)]
+        south = [jnp.where(column > 0, near, far) for near, far in zip(before, before_far)]
         return north, south
 
-    pad_ref[...] = jnp.zeros_like(pad_ref)
+    def cleared(tiles):
+        return [jnp.where(at_left, zero, tiles[0]), tiles[1], tiles[2], jnp.where(at_right, zero, tiles[3])]
+
+    def part(n):
+        return cleared(
+            [
+                left_ref[8 * n : 8 * n + 8, :],
+                part_ref[pl.ds(16 * n, 8, stride=2), :],
+                part_ref[pl.ds(16 * n + 1, 8, stride=2), :],
+                right_ref[8 * n : 8 * n + 8, :],
+            ]
+        )
+
+    item = lane % 64
+    end_lane = jnp.where(item < 16, item + (W - 16), jnp.where(item < 32, item - 16, 0))
+    side_lane = jnp.clip(jnp.where(item < 48, (item - 33) * 16 + 15, (item - 49) * 16), 0, W - 1)
+    corner_lane = jnp.where(item < 40, W - 1, jnp.where(item < 45, 15, jnp.where(item < 52, W - 16, 0)))
+    is_corner = (item == 32) | (item == 41) | (item == 48) | (item == 57)
+
+    def picked(values, index):
+        return jnp.take_along_axis(values, index, axis=1)
+
     for r in range(3):
-        send_ref[pl.ds(r, 8, stride=3), :] = jnp.zeros((8, W), F32)
-
-    lane8 = lanes(8)
-    item = lane8 % 64
-    west_east = jnp.where(item < 16, item + 112, item - 16)
-    west_east = jnp.where(item < 32, west_east, 0)
-    left_column = item - 33
-    right_column = item - 49
-    side = jnp.where(item < 48, left_column * 16 + 15, right_column * 16)
-    side = jnp.clip(side, 0, W - 1)
-
-    coarse = part_ref[0:64, :]
+        send_ref[pl.ds(r, 8, stride=3), :] = zero
+    coarse = part(0)
     for n in range(1, 8):
-        east, west = shifted(coarse)
-        north, south = shifted_y(coarse)
-        slope = along_x * (east - west) + along_y * (north - south)
-        image = coarse + (spread * ((east + west) + (north + south) - 4.0 * coarse) - coarse * slope)
-        for g in range(8):
-            start = (g + 1) * 24 + 8
-            pad_ref[start : start + 8, :] = image[8 * g : 8 * g + 8]
-
-        def tiles(dx, b):
-            return pad_ref[pl.ds((1 + dx) * 24 + 8 + b, 8, stride=24), :]
-
-        b = 2 * gy
+        north, south = along_columns(coarse)
+        image = []
+        for b in range(4):
+            east, west = along_rows(coarse[b], *neighbours(coarse[b]))
+            slope = along_x * (east - west) + along_y * (north[b] - south[b])
+            total = (east + west) + (north[b] + south[b])
+            image.append(coarse[b] + (spread * (total - 4.0 * coarse[b]) - coarse[b] * slope))
+        image = cleared(image)
+        beside = [neighbours(tile) for tile in image]
+
         rows = []
-        for h in range(2):
-            ends = jnp.where(lane8 >= 64, tiles(-1, b + h), tiles(1, b + h))
-            ends = jnp.take_along_axis(ends, west_east, axis=1)
-            sides = []
-            for away in (-1, 1):
-                own = jnp.take_along_axis(tiles(0, b + h + away), side, axis=1)
-                at = 15 if away < 0 else 0
-                lower = jnp.take_along_axis(tiles(-1, b + h + away), jnp.full((8, W), 112 + at, jnp.int32), axis=1)
-                upper = jnp.take_along_axis(tiles(1, b + h + away), jnp.full((8, W), at, jnp.int32), axis=1)
-                first = 32 if away < 0 else 48
-                value = jnp.where(item == first, lower, jnp.where(item == first + 9, upper, own))
-                sides.append(value)
-            rows.append(jnp.where(item < 32, ends, jnp.where(item < 48, sides[0], sides[1])))
+        for b in (1, 2):
+            ends = picked(jnp.where(lane >= 64, beside[b][1], beside[b][0]), end_lane)
+            sides = picked(jnp.where(column == 15, image[b - 1], image[b + 1]), side_lane)
+            corners = jnp.where(
+                lane >= 64,
+                jnp.where(column == 15, beside[b - 1][1], beside[b + 1][1]),
+                jnp.where(column == 15, beside[b - 1][0], beside[b + 1][0]),
+            )
+            corners = picked(corners, corner_lane)
+            rows.append(jnp.where(item < 32, ends, jnp.where(is_corner, corners, sides)))
         base = n * 24
-        send_ref[pl.ds(base, 8, stride=3), :] = tiles(0, b)
-        send_ref[pl.ds(base + 1, 8, stride=3), :] = tiles(0, b + 1)
-        send_ref[pl.ds(base + 2, 8, stride=3), :] = jnp.where(lane8 < 64, rows[0], rows[1])
+        send_ref[pl.ds(base, 8, stride=3), :] = image[1]
+        send_ref[pl.ds(base + 1, 8, stride=3), :] = image[2]
+        send_ref[pl.ds(base + 2, 8, stride=3), :] = jnp.where(lane < 64, rows[0], rows[1])
 
         if n < 7:
-            east, west = shifted(image)
-            blended = BLEND[0] * west + BLEND[1] * image + BLEND[2] * east
-            north, south = shifted_y(blended)
-            blended = BLEND[0] * south + BLEND[1] * blended + BLEND[2] * north
-            coarse = part_ref[n * 64 : (n + 1) * 64, :] + blended
+            blended = []
+            for tile, pair in zip(image, beside):
+                east, west = along_rows(tile, *pair)
+                blended.append(BLEND[0] * west + BLEND[1] * tile + BLEND[2] * east)
+            north, south = along_columns(blended)
+            coarse = cleared(
+                [
+                    value + (BLEND[0] * s + BLEND[1] * tile + BLEND[2] * n_)
+                    for value, s, tile, n_ in zip(part(n), south, blended, north)
+                ]
+            )
 
 
 def end_kernel(place_ref, end_ref, image_ref, back_ref, out_ref, change_ref, along_ref, fine_ref, turn_ref):
@@ -465,7 +484,7 @@
     right = ring(first_columns, "gy", -1)
     fine_end, image, parts = call(
         fine_kernel,
-        (shape(NX * HALF), shape(10 * OROWS), shape(8 * LEVELS)),
+        (shape(NX * HALF), shape(10 * OROWS), shape(2 * LEVELS)),
         [SMEM] + [VMEM] * 7,
         [
             scratch(40 * FROWS), scratch(40 * FROWS), scratch(FROWS), scratch(12 * CROWS),
@@ -473,11 +492,14 @@
         ],
         "fine",
     )(place, turned, west, east, left, right, diffusivity.reshape(1, LEVELS), wind)
-    parts = lax.all_to_all(parts.reshape(256, 2, W), ("tm", "gx", "gy"), 0, 0, tiled=True)
-    images = call(chain_kernel, shape(3 * 64), [SMEM, SMEM, SMEM, VMEM], [scratch(10 * 24)], "chain")(
-        place, diffusivity, wind, parts.reshape(512, W)
+    parts = lax.all_to_all(parts.reshape(LEVELS, 2, W), ("tm", "gx"), 0, 0, tiled=True).reshape(2 * LEVELS, W)
+    first_half, second_half = call(split_kernel, (shape(LEVELS), shape(LEVELS)), [VMEM], [], "split")(parts)
+    left = ring(second_half, "gy", 1)
+    right = ring(first_half, "gy", -1)
+    images = call(chain_kernel, shape(3 * LEVELS), [SMEM] * 3 + [VMEM] * 3, [], "chain")(
+        place, diffusivity, wind, parts, left, right
     )
-    images = lax.all_to_all(images.reshape(64, 3, W), ("tm", "gx"), 0, 0, tiled=True)
+    images = lax.all_to_all(images.reshape(LEVELS, 3, W), ("tm", "gx"), 0, 0, tiled=True)
     ending = call(
         end_kernel,
         shape(LEVELS * NX),

time: 69.1 us -> 66 us (0.955)
  blocking collectives: 45.5 us -> 38.8 us
  starting transfers between devices: 6.03 us -> 8.7 us
  waiting for transfers between devices: 5.9 us -> 7.29 us
    all_to_all x2, blocking collectives: 45.5 us -> 38.8 us  [the longest x1 22.3 us: shards(): lax.all_to_all(parts.reshape(LEVELS, 2, W), ('tm', 'gx'), 0, 0, tiled=True)]
    ppermute x4 -> x6, starting transfers between devices: 6.03 us -> 8.7 us  [ring(): lax.ppermute(array, axis, [(i, (i + distance) % devices) for i in range(d...]
    ppermute x4 -> x6, waiting for transfers between devices: 5.9 us -> 7.29 us  [ring(): lax.ppermute(array, axis, [(i, (i + distance) % devices) for i in range(d...]
    pallas_call x2 -> x3, Pallas kernels: 5.98 us -> 5.62 us  [the longest x1 3.41 us: shards(): call(fine_kernel, (shape(NX * HALF), shape(10 * OROWS), shape(2 * LEVELS)...]
  transfers between devices with their start and end apart: 4 -> 6, of which waited for: 3 -> 5; matrix products, arithmetic and copies ran while one was open for 0% -> 0% of each run, Pallas kernels for 0% -> 0%
where the time goes in v2:
time: 66 us; the launch traced here: 65.8 us
  blocking collectives  38.8 us (59%)
  Pallas kernels  9.64 us (15%)
  starting transfers between devices  8.7 us (13%)
  waiting for transfers between devices  7.29 us (11%)
  local copies, waits for them, and re-layouts  1.32 us (2%)
    all_to_all x1, blocking collectives, shards(): lax.all_to_all(parts.reshape(LEVELS, 2, W), ('tm', 'gx'), 0, 0, tiled=True)  22.3 us
    all_to_all x1, blocking collectives, shards(): lax.all_to_all(images.reshape(LEVELS, 3, W), ('tm', 'gx'), 0, 0, tiled=True)  16.4 us
    ppermute x6, starting transfers between devices, ring(): lax.ppermute(array, axis, [(i, (i + distance) % devices) for i in range(d...  8.7 us
    ppermute x6, waiting for transfers between devices, ring(): lax.ppermute(array, axis, [(i, (i + distance) % devices) for i in range(d...  7.29 us
    pallas_call x1, Pallas kernels, shards(): call(fine_kernel, (shape(NX * HALF), shape(10 * OROWS), shape(2 * LEVELS)...  3.41 us
    pallas_call x1, Pallas kernels, shards(): call(end_kernel, shape(LEVELS * NX), [SMEM] + [VMEM] * 3, [scratch(10 * O...  2.93 us
    pallas_call x1, Pallas kernels, shards(): call(chain_kernel, shape(3 * LEVELS), [SMEM] * 3 + [VMEM] * 3, [], 'chain')  2.21 us
  transfers between devices with their start and end apart: 6, of which 5 were waited for; matrix products, arithmetic and copies ran while one was open for 0% of the time, Pallas kernels for 0%

profile of v2, /device:TPU:1, one launch (start us, length us, event | category | flops | bytes accessed | tf_op | source)
XLA Modules:
  0.0 65.8 jit_solution(15875074832453741573)
XLA Ops:
  0.0 0.0 copy-start
  0.0 1.2 %copy-done = f32[1,64,32,128]{3,2,1,0:T(8,128)S(1)} copy-done((f32[1,64,32,128]{3,2,1,0:T(8,128)S(1)}, f32[1,64,32,128]{3,2,1,0:T(8,128)}, u32[]{:S(2)}) %copy-start) | copy-done | bytes 1048600
  1.2 1.0 %pack.1 = (f32[2048,128]{1,0:T(8,128)S(1)}, f32[272,128]{1,0:T(8,128)S(1)}, f32[272,128]{1,0:T(8,128)S(1)}) custom-call(f32[2048,128]{1,0:T(8,128)S(1)} %bitcast.8), custom_call_target="tpu_custom_call" | custom-call | tf_op jit(solution)/shard_map/pack/pallas_call | solution.py:475
  2.2 2.6 %collective-permute-start = (f32[272,128]{1,0:T(8,128)S(1)}, f32[272,128]{1,0:T(8,128)S(1)}, u32[]{:S(2)}, u32[]{:S(2)}) collective-permute-start(f32[272,128]{1,0:T(8,128)S(1)} %get-tuple-element.16), channel_id=1, source_target_pairs={{0,4},{4,8},{8,12},{12,16},{16,20},{20,24},{24,28},{28,0},{1,5},{5... | collective-permute-start | bytes 417800 | tf_op jit(solution)/shard_map/ppermute | solution.py:469
  4.8 0.7 %collective-permute-start.1 = (f32[272,128]{1,0:T(8,128)S(1)}, f32[272,128]{1,0:T(8,128)S(1)}, u32[]{:S(2)}, u32[]{:S(2)}) collective-permute-start(f32[272,128]{1,0:T(8,128)S(1)} %get-tuple-element.17), channel_id=1, source_target_pairs={{0,28},{4,0},{8,4},{12,8},{16,12},{20,16},{24,20},{28,24},{1,29},{... | collective-permute-start | bytes 417800 | tf_op jit(solution)/shard_map/ppermute | solution.py:469
  5.5 1.4 %collective-permute-done.west_ref = f32[272,128]{1,0:T(8,128)S(1)} collective-permute-done((f32[272,128]{1,0:T(8,128)S(1)}, f32[272,128]{1,0:T(8,128)S(1)}, u32[]{:S(2)}, u32[]{:S(2)}) %collective-permute-start) | collective-permute-done | bytes 139296 | tf_op jit(solution)/shard_map/ppermute | solution.py:469
  6.8 2.8 %collective-permute-done.1.east_ref = f32[272,128]{1,0:T(8,128)S(1)} collective-permute-done((f32[272,128]{1,0:T(8,128)S(1)}, f32[272,128]{1,0:T(8,128)S(1)}, u32[]{:S(2)}, u32[]{:S(2)}) %collective-permute-start.1) | collective-permute-done | bytes 139296 | tf_op jit(solution)/shard_map/ppermute | solution.py:469
  9.6 0.1 sides.1
  9.7 1.1 %collective-permute-start.2 = (f32[168,128]{1,0:T(8,128)S(1)}, f32[168,128]{1,0:T(8,128)S(1)}, u32[]{:S(2)}, u32[]{:S(2)}) collective-permute-start(f32[168,128]{1,0:T(8,128)S(1)} %get-tuple-element.18), channel_id=1, source_target_pairs={{0,1},{1,2},{2,3},{3,0},{4,5},{5,6},{6,7},{7,4},{8,9},{9,10},{10,1... | collective-permute-start | bytes 258056 | tf_op jit(solution)/shard_map/ppermute | solution.py:469
  10.8 1.7 %collective-permute-start.3 = (f32[168,128]{1,0:T(8,128)S(1)}, f32[168,128]{1,0:T(8,128)S(1)}, u32[]{:S(2)}, u32[]{:S(2)}) collective-permute-start(f32[168,128]{1,0:T(8,128)S(1)} %get-tuple-element.19), channel_id=1, source_target_pairs={{0,3},{1,0},{2,1},{3,2},{4,7},{5,4},{6,5},{7,6},{8,11},{9,8},{10,9... | collective-permute-start | bytes 258056 | tf_op jit(solution)/shard_map/ppermute | solution.py:469
  12.5 0.1 pad_add_fusion.place_ref
  12.5 0.0 copy-start.1
  12.5 0.0 copy-start.2
  12.5 1.8 %collective-permute-done.2.left_ref = f32[168,128]{1,0:T(8,128)S(1)} collective-permute-done((f32[168,128]{1,0:T(8,128)S(1)}, f32[168,128]{1,0:T(8,128)S(1)}, u32[]{:S(2)}, u32[]{:S(2)}) %collective-permute-start.2) | collective-permute-done | bytes 86048 | tf_op jit(solution)/shard_map/ppermute | solution.py:469
  14.3 0.0 collective-permute-done.3.right_ref
  14.3 0.0 copy-done.1
  14.3 0.0 copy-done.2
  14.3 3.4 %fine.1 = (f32[2048,128]{1,0:T(8,128)S(1)}, f32[240,128]{1,0:T(8,128)S(1)}, f32[128,128]{1,0:T(8,128)S(1)}) custom-call(s32[3]{0:T(128)S(1)} %pad_add_fusion.place_ref, f32[2048,128]{1,0:T(8,128)S(1)} %get-tuple-element.15.t_ref, f32[272,128]{1,0:T(8,128)S(1)} %collective-permute-done.west_ref, f32[272,128]{1,0:T(8,128)S(1)} %collective-permute-done.1.east_ref, ...), custom_call_target="tpu_custom_call" | custom-call | tf_op jit(solution)/shard_map/fine/pallas_call | solution.py:485
  17.8 22.3 %all_to_all.10 = f32[64,2,128]{2,1,0:T(2,128)S(1)} all-to-all(f32[64,2,128]{2,1,0:T(2,128)S(1)} %bitcast.11), channel_id=1, replica_groups=mesh['tm'=8,'gx'=8,'gy'=4] {'tm','gx'}, dimensions={0} | all-to-all | bytes 131072 | tf_op jit(solution)/shard_map/all_to_all | solution.py:495
  40.1 1.3 %collective-permute-start.4 = (f32[64,128]{1,0:T(8,128)S(1)}, f32[64,128]{1,0:T(8,128)S(1)}, u32[]{:S(2)}, u32[]{:S(2)}) collective-permute-start(f32[64,128]{1,0:T(8,128)S(1)} %get-tuple-element.23), channel_id=1, source_target_pairs={{0,1},{1,2},{2,3},{3,0},{4,5},{5,6},{6,7},{7,4},{8,9},{9,10},{10,1... | collective-permute-start | bytes 98312 | tf_op jit(solution)/shard_map/ppermute | solution.py:469
  41.4 1.4 %collective-permute-start.5 = (f32[64,128]{1,0:T(8,128)S(1)}, f32[64,128]{1,0:T(8,128)S(1)}, u32[]{:S(2)}, u32[]{:S(2)}) collective-permute-start(f32[64,128]{1,0:T(8,128)S(1)} %get-tuple-element.24), channel_id=1, source_target_pairs={{0,3},{1,0},{2,1},{3,2},{4,7},{5,4},{6,5},{7,6},{8,11},{9,8},{10,9... | collective-permute-start | bytes 98312 | tf_op jit(solution)/shard_map/ppermute | solution.py:469
  42.8 1.3 %collective-permute-done.4.left_ref = f32[64,128]{1,0:T(8,128)S(1)} collective-permute-done((f32[64,128]{1,0:T(8,128)S(1)}, f32[64,128]{1,0:T(8,128)S(1)}, u32[]{:S(2)}, u32[]{:S(2)}) %collective-permute-start.4) | collective-permute-done | bytes 32800 | tf_op jit(solution)/shard_map/ppermute | solution.py:469
  44.1 0.1 collective-permute-done.5.right_ref
  44.2 2.2 %chain.1 = f32[192,128]{1,0:T(8,128)S(1)} custom-call(s32[3]{0:T(128)S(1)} %pad_add_fusion.place_ref, f32[64]{0:T(128)S(1)} %copy-done.2, f32[2,64]{1,0:T(2,128)S(1)} %copy-done.1, f32[128,128]{1,0:T(8,128)S(1)} %bitcast.10, f32[64,128]{1,0:T(8,128)S(1)} %collective-permute-done.4.left_ref, f32[64,128]{1,0:T(8,128)S(1)} %collective-permute-done.5.right_ref), custom_call_target="tpu_custom_call" | custom-call | tf_op jit(solution)/shard_map/chain/pallas_call | solution.py:499
  46.4 16.4 %all_to_all.11 = f32[64,3,128]{2,1,0:T(4,128)S(1)} all-to-all(f32[64,3,128]{2,1,0:T(4,128)S(1)} %reshape.25), channel_id=1, replica_groups=mesh['tm'=8,'gx'=8,'gy'=4] {'tm','gx'}, dimensions={0} | all-to-all | bytes 196608 | tf_op jit(solution)/shard_map/all_to_all | solution.py:502
  62.9 2.9 %ending.1 = f32[2048,128]{1,0:T(8,128)} custom-call(s32[3]{0:T(128)S(1)} %pad_add_fusion.place_ref, f32[2048,128]{1,0:T(8,128)S(1)} %get-tuple-element.20.end_ref, f32[240,128]{1,0:T(8,128)S(1)} %get-tuple-element.21.image_ref, f32[192,128]{1,0:T(8,128)S(1)} %reshape.26.back_ref), custom_call_target="tpu_custom_call" | custom-call | tf_op jit(solution)/shard_map/ending/pallas_call | solution.py:503
  (3 shorter events, 0.1 us)
Async XLA Ops:
  0.0 1.2 %copy-start = (f32[1,64,32,128]{3,2,1,0:T(8,128)S(1)}, f32[1,64,32,128]{3,2,1,0:T(8,128)}, u32[]{:S(2)}) copy-start(f32[1,64,32,128]{3,2,1,0:T(8,128)} %param.3) | copy-start | bytes 3145732
  2.2 4.6 %collective-permute-start = (f32[272,128]{1,0:T(8,128)S(1)}, f32[272,128]{1,0:T(8,128)S(1)}, u32[]{:S(2)}, u32[]{:S(2)}) collective-permute-start(f32[272,128]{1,0:T(8,128)S(1)} %get-tuple-element.16), channel_id=1, source_target_pairs={{0,4},{4,8},{8,12},{12,16},{16,20},{20,24},{24,28},{28,0},{1,5},{5... | collective-permute-start | bytes 417800 | tf_op jit(solution)/shard_map/ppermute | solution.py:469
  4.8 4.8 %collective-permute-start.1 = (f32[272,128]{1,0:T(8,128)S(1)}, f32[272,128]{1,0:T(8,128)S(1)}, u32[]{:S(2)}, u32[]{:S(2)}) collective-permute-start(f32[272,128]{1,0:T(8,128)S(1)} %get-tuple-element.17), channel_id=1, source_target_pairs={{0,28},{4,0},{8,4},{12,8},{16,12},{20,16},{24,20},{28,24},{1,29},{... | collective-permute-start | bytes 417800 | tf_op jit(solution)/shard_map/ppermute | solution.py:469
  9.7 4.6 %collective-permute-start.2 = (f32[168,128]{1,0:T(8,128)S(1)}, f32[168,128]{1,0:T(8,128)S(1)}, u32[]{:S(2)}, u32[]{:S(2)}) collective-permute-start(f32[168,128]{1,0:T(8,128)S(1)} %get-tuple-element.18), channel_id=1, source_target_pairs={{0,1},{1,2},{2,3},{3,0},{4,5},{5,6},{6,7},{7,4},{8,9},{9,10},{10,1... | collective-permute-start | bytes 258056 | tf_op jit(solution)/shard_map/ppermute | solution.py:469
  10.8 3.5 %collective-permute-start.3 = (f32[168,128]{1,0:T(8,128)S(1)}, f32[168,128]{1,0:T(8,128)S(1)}, u32[]{:S(2)}, u32[]{:S(2)}) collective-permute-start(f32[168,128]{1,0:T(8,128)S(1)} %get-tuple-element.19), channel_id=1, source_target_pairs={{0,3},{1,0},{2,1},{3,2},{4,7},{5,4},{6,5},{7,6},{8,11},{9,8},{10,9... | collective-permute-start | bytes 258056 | tf_op jit(solution)/shard_map/ppermute | solution.py:469
  12.5 1.8 %copy-start.1 = (f32[2,64]{1,0:T(2,128)S(1)}, f32[2,64]{1,0:T(2,128)}, u32[]{:S(2)}) copy-start(f32[2,64]{1,0:T(2,128)} %wind_ref.3) | copy-start | bytes 1540
  12.5 1.8 %copy-start.2 = (f32[64]{0:T(128)S(1)}, f32[64]{0:T(128)}, u32[]{:S(2)}) copy-start(f32[64]{0:T(128)} %diffuse_ref.1) | copy-start | bytes 772
  40.1 4.0 %collective-permute-start.4 = (f32[64,128]{1,0:T(8,128)S(1)}, f32[64,128]{1,0:T(8,128)S(1)}, u32[]{:S(2)}, u32[]{:S(2)}) collective-permute-start(f32[64,128]{1,0:T(8,128)S(1)} %get-tuple-element.23), channel_id=1, source_target_pairs={{0,1},{1,2},{2,3},{3,0},{4,5},{5,6},{6,7},{7,4},{8,9},{9,10},{10,1... | collective-permute-start | bytes 98312 | tf_op jit(solution)/shard_map/ppermute | solution.py:469
  41.4 2.8 %collective-permute-start.5 = (f32[64,128]{1,0:T(8,128)S(1)}, f32[64,128]{1,0:T(8,128)S(1)}, u32[]{:S(2)}, u32[]{:S(2)}) collective-permute-start(f32[64,128]{1,0:T(8,128)S(1)} %get-tuple-element.24), channel_id=1, source_target_pairs={{0,3},{1,0},{2,1},{3,2},{4,7},{5,4},{6,5},{7,6},{8,11},{9,8},{10,9... | collective-permute-start | bytes 98312 | tf_op jit(solution)/shard_map/ppermute | solution.py:469

commit v3 on v2

v3 whole, which is shorter than its diff:
```python
import jax
import jax.numpy as jnp
import ml_dtypes
import numpy as np
from jax import lax
from jax.experimental import pallas as pl
from jax.experimental.pallas import tpu as pltpu
from jax.sharding import PartitionSpec as P

SUB = 4
STEP = 0.2
LEVELS = 64
NX = 32
HALF = 64
CX = NX // 4
CY = HALF // 4
W = 128
WEIGHTS_LOW = (0.375, 0.125, 0.0, 0.0)
WEIGHTS_MID = (0.625, 0.875, 0.875, 0.625)
WEIGHTS_HIGH = (0.0, 0.0, 0.125, 0.375)
BLEND = (0.125, 0.75, 0.125)
F32 = jnp.float32

STRIP = 4 * HALF + CY
SIDE = 20 * 8 + 8
FROWS = 88
CROWS = 40
OROWS = 24


def lanes(rows):
    return lax.broadcasted_iota(jnp.int32, (rows, W), 1)


def rows_of(rows):
    return lax.broadcasted_iota(jnp.int32, (rows, W), 0)


def low(rows):
    return lanes(rows) < LEVELS


def swap(value):
    return pltpu.roll(value, LEVELS, 1)


def coarse_rows(ref, start, count):
    total = ref[pl.ds(start, count, stride=4), :]
    for offset in range(1, 4):
        total = total + ref[pl.ds(start + offset, count, stride=4), :]
    return total * (1.0 / 16.0)


def turned_pair(rows_ref, x, stride):
    lo = low(HALF)
    both = jnp.concatenate(
        [rows_ref[pl.ds(x, LEVELS, stride=stride), :], rows_ref[pl.ds(x + 1, LEVELS, stride=stride), :]], axis=0
    ).T
    top = both[:HALF]
    bottom = both[HALF:]
    return jnp.where(lo, top, swap(bottom)), jnp.where(lo, swap(top), bottom)


def edge_kernel(low_ref, high_ref, edge_ref, first_ref, last_ref, sum_ref):
    for side, (rows_ref, strip_ref) in enumerate(((low_ref, first_ref), (high_ref, last_ref))):
        rows = []
        for x in range(0, 8, 2):
            rows += turned_pair(rows_ref, x, 8)
        for x in range(8):
            base = (8 * side + x) * HALF
            edge_ref[base : base + HALF, :] = rows[x]
        near = rows[:4] if side == 0 else rows[4:]
        far = rows[4:] if side == 0 else rows[:4]
        for x in range(4):
            strip_ref[x * HALF : (x + 1) * HALF, :] = near[x]
        sum_ref[...] = (far[0] + far[1]) + (far[2] + far[3])
        strip_ref[4 * HALF :, :] = coarse_rows(sum_ref, 0, CY)


def middle_kernel(rows_ref, middle_ref):
    for x in range(0, 16, 2):
        one, two = turned_pair(rows_ref, x, 16)
        middle_ref[x * HALF : (x + 1) * HALF, :] = one
        middle_ref[(x + 1) * HALF : (x + 2) * HALF, :] = two


def block_row(x, edge_ref, middle_ref, west_ref, east_ref):
    if x < 0:
        return west_ref, (x + 4) * HALF
    if x >= NX:
        return east_ref, (x - NX) * HALF
    if x < 8:
        return edge_ref, x * HALF
    if x >= NX - 8:
        return edge_ref, (x - NX + 16) * HALF
    return middle_ref, (x - 8) * HALF


def side_kernel(edge_ref, middle_ref, west_ref, east_ref, left_ref, right_ref):
    lo = low(8)

    def edge(x, start):
        source, base = block_row(x, edge_ref, middle_ref, west_ref, east_ref)
        return source[base + start : base + start + 8, :]

    for i in range(20):
        left_ref[8 * i : 8 * i + 8, :] = jnp.where(lo, edge(i - 4, 0), swap(edge(i + 16, 0)))
        right_ref[8 * i : 8 * i + 8, :] = jnp.where(
            lo, swap(edge(i - 4, HALF - 8)), edge(i + 16, HALF - 8)
        )
    base = 4 * HALF
    left_ref[160:168, :] = jnp.where(lo, west_ref[base : base + 8, :], swap(east_ref[base : base + 8, :]))
    right_ref[160:168, :] = jnp.where(
        lo, swap(west_ref[base + 8 : base + 16, :]), east_ref[base + 8 : base + 16, :]
    )


def both_halves(values):
    return jnp.concatenate([values, values], axis=1)


def coefficients(diffuse_ref, wind_ref):
    diffuse = both_halves(diffuse_ref[...])
    wind = both_halves(wind_ref[...])
    spread = jnp.broadcast_to(STEP * diffuse, (8, W))
    along_x = jnp.broadcast_to((0.5 * STEP) * wind[0:1], (8, W))
    along_y = jnp.broadcast_to((0.5 * STEP) * wind[1:2], (8, W))
    return spread, along_x, along_y


def advanced(ref, r, rows, coefs, factor):
    spread, along_x, along_y = coefs
    centre = ref[r : r + 8, :]
    east = ref[r + rows : r + rows + 8, :]
    west = ref[r - rows : r - rows + 8, :]
    north = ref[r + 1 : r + 9, :]
    south = ref[r - 1 : r + 7, :]
    slope = along_x * (east - west) + along_y * (north - south)
    return centre + ((factor * spread) * ((east + west) + (north + south) - 4.0 * centre) - centre * slope)


def substeps(place_ref, states, end_ref, coefs, tiles, end_tiles):
    at_west = place_ref[1] == 0
    at_east = place_ref[1] == 7
    lo = low(8)
    zero8 = jnp.zeros((8, W), F32)
    left_out = jnp.logical_and(place_ref[2] == 0, jnp.logical_and(rows_of(8) < 4, lo))
    right_out = jnp.logical_and(place_ref[2] == 3, jnp.logical_and(rows_of(8) >= 4, jnp.logical_not(lo)))
    for step in range(SUB - 1):
        for tile in tiles:
            for i in range(step + 1, 39 - step):
                r = i * FROWS + 8 + 8 * tile
                value = advanced(states[step], r, FROWS, coefs, 1.0)
                if tile == 0:
                    value = jnp.where(left_out, zero8, value)
                if tile == 8:
                    value = jnp.where(right_out, zero8, value)
                if i < 4:
                    value = jnp.where(at_west, zero8, value)
                if i >= 36:
                    value = jnp.where(at_east, zero8, value)
                states[step + 1][r : r + 8, :] = value
    for tile in end_tiles:
        for i in range(4, 36):
            o = (i - 4) * HALF + 8 * tile
            end_ref[o : o + 8, :] = advanced(states[SUB - 1], i * FROWS + 12 + 8 * tile, FROWS, coefs, 1.0)


def inner_kernel(
    place_ref, edge_ref, middle_ref, west_ref, east_ref, diffuse_ref, wind_ref,
    s0_ref, s1_ref, s2_ref, s3_ref, end_ref, coarse_ref, sum_ref,
):
    lo8 = low(8)
    zero8 = jnp.zeros((8, W), F32)
    for i in range(40):
        source, base = block_row(i - 4, edge_ref, middle_ref, west_ref, east_ref)
        rows = source[base : base + HALF, :]
        before = jnp.where(lo8, zero8, swap(rows[HALF - 8 :]))
        after = jnp.where(lo8, swap(rows[:8]), zero8)
        if i < 4 or i >= 36:
            outside = place_ref[1] == (0 if i < 4 else 7)
            rows = jnp.where(outside, jnp.zeros_like(rows), rows)
            before = jnp.where(outside, zero8, before)
            after = jnp.where(outside, zero8, after)
        start = i * FROWS
        s0_ref[start : start + 4, :] = zero8[:4]
        s0_ref[start + 4 : start + 12, :] = before
        s0_ref[start + 12 : start + 76, :] = rows
        s0_ref[start + 76 : start + 84, :] = after
        s0_ref[start + 84 : start + 88, :] = zero8[:4]

    coarse_ref[...] = jnp.zeros_like(coarse_ref)
    for j in range(10):
        base = 4 * j * FROWS
        sum_ref[...] = (s0_ref[base : base + FROWS, :] + s0_ref[base + FROWS : base + 2 * FROWS, :]) + (
            s0_ref[base + 2 * FROWS : base + 3 * FROWS, :] + s0_ref[base + 3 * FROWS : base + 4 * FROWS, :]
        )
        start = (j + 1) * CROWS
        coarse_ref[start + 7 : start + 27, :] = coarse_rows(sum_ref, 4, 20)

    states = (s0_ref, s1_ref, s2_ref, s3_ref)
    substeps(place_ref, states, end_ref, coefficients(diffuse_ref, wind_ref), range(9), range(8))


def outer_kernel(
    place_ref, west_ref, east_ref, left_ref, right_ref, diffuse_ref, wind_ref,
    s0_in, s1_in, s2_in, s3_in, end_in, coarse_in,
    s0_ref, s1_ref, s2_ref, s3_ref, end_ref, coarse_ref, change_ref, send_ref,
    sum_ref, blend_ref, part_ref,
):
    del s0_in, s1_in, s2_in, s3_in, end_in, coarse_in
    first_segment = place_ref[0] == 0
    at_west = place_ref[1] == 0
    at_east = place_ref[1] == 7
    at_left = place_ref[2] == 0
    at_right = place_ref[2] == 3
    lo8 = low(8)
    zero8 = jnp.zeros((8, W), F32)
    coefs = coefficients(diffuse_ref, wind_ref)

    for j in range(10):
        befores = []
        afters = []
        for i in range(4 * j, 4 * j + 4):
            k = i % 20
            from_left = left_ref[8 * k : 8 * k + 8, :]
            from_right = right_ref[8 * k : 8 * k + 8, :]
            if i >= 20:
                from_left = swap(from_left)
            else:
                from_right = swap(from_right)
            start = i * FROWS
            known = s0_ref[start + 4 : start + 12, :]
            before = jnp.where(lo8, jnp.where(at_left, zero8, from_left), known)
            known = s0_ref[start + 76 : start + 84, :]
            after = jnp.where(lo8, known, jnp.where(at_right, zero8, from_right))
            if i < 4 or i >= 36:
                outside = at_west if i < 4 else at_east
                before = jnp.where(outside, zero8, before)
                after = jnp.where(outside, zero8, after)
            s0_ref[start + 4 : start + 12, :] = before
            s0_ref[start + 76 : start + 84, :] = after
            befores.append(before)
            afters.append(after)
        base = 16 * j
        sum_ref[base : base + 8, :] = (befores[0] + befores[1]) + (befores[2] + befores[3])
        sum_ref[base + 8 : base + 16, :] = (afters[0] + afters[1]) + (afters[2] + afters[3])
        start = (j + 1) * CROWS
        coarse_ref[start + 7 : start + 9, :] = coarse_rows(sum_ref, base, 2)
        coarse_ref[start + 25 : start + 27, :] = coarse_rows(sum_ref, base + 8, 2)
    left_corner = left_ref[160:168, :]
    right_corner = right_ref[160:168, :]
    for source, start, outside, is_west in (
        (west_ref, 0, at_west, True),
        (east_ref, 11 * CROWS, at_east, False),
    ):
        rows = source[4 * HALF :, :]
        from_left = left_corner if is_west else swap(left_corner)
        from_right = swap(right_corner) if is_west else right_corner
        from_left = jnp.where(at_left, zero8, from_left)
        from_right = jnp.where(at_right, zero8, from_right)
        before = jnp.where(lo8, from_left, swap(rows[8:]))
        after = jnp.where(lo8, swap(rows[:8]), from_right)
        coarse_ref[start + 1 : start + 9, :] = jnp.where(outside, zero8, before)
        coarse_ref[start + 9 : start + 25, :] = jnp.where(outside, jnp.zeros_like(rows), rows)
        coarse_ref[start + 25 : start + 33, :] = jnp.where(outside, zero8, after)

    for j in range(10):
        for tile in range(3):
            image = advanced(coarse_ref, (j + 1) * CROWS + 8 + 8 * tile, CROWS, coefs, 0.25)
            cy = rows_of(8) + (8 * tile - 1)
            outside = cy > CY
            if tile == 0:
                outside = jnp.logical_or(outside, jnp.logical_and(at_left, jnp.logical_and(cy < 0, lo8)))
            if tile == 2:
                outside = jnp.logical_or(
                    outside, jnp.logical_and(at_right, jnp.logical_and(cy >= CY, jnp.logical_not(lo8)))
                )
            if j == 0:
                outside = jnp.logical_or(outside, at_west)
            if j == 9:
                outside = jnp.logical_or(outside, at_east)
            image = jnp.where(outside, zero8, image)
            o = j * OROWS + 8 * tile
            change_ref[o : o + 8, :] = jnp.where(first_segment, image, zero8) - image

    states = (s0_ref, s1_ref, s2_ref, s3_ref)
    substeps(place_ref, states, end_ref, coefs, (0, 8), (0, 7))

    for j in range(CX):
        lower = change_ref[j * OROWS : (j + 1) * OROWS, :]
        middle = change_ref[(j + 1) * OROWS : (j + 2) * OROWS, :]
        upper = change_ref[(j + 2) * OROWS : (j + 3) * OROWS, :]
        slot = j * OROWS
        blend_ref[slot : slot + OROWS, :] = BLEND[0] * lower + BLEND[1] * middle + BLEND[2] * upper
        blended = (
            BLEND[0] * blend_ref[slot : slot + CY, :]
            + BLEND[1] * blend_ref[slot + 1 : slot + CY + 1, :]
            + BLEND[2] * blend_ref[slot + 2 : slot + CY + 2, :]
        )
        base = 4 * j * HALF
        total = (end_ref[base : base + HALF, :] + end_ref[base + HALF : base + 2 * HALF, :]) + (
            end_ref[base + 2 * HALF : base + 3 * HALF, :] + end_ref[base + 3 * HALF : base + 4 * HALF, :]
        )
        spot = 160 + j * HALF
        sum_ref[spot : spot + HALF, :] = total
        part_ref[j * CY : (j + 1) * CY, :] = coarse_rows(sum_ref, spot, CY) + blended
    turned = part_ref[...].T
    for h in range(2):
        send_ref[pl.ds(h, LEVELS, stride=2), :] = turned[h * LEVELS : (h + 1) * LEVELS]


def split_kernel(part_ref, first_ref, second_ref):
    first_ref[...] = part_ref[pl.ds(0, LEVELS, stride=2), :]
    second_ref[...] = part_ref[pl.ds(1, LEVELS, stride=2), :]


def chain_kernel(place_ref, diffuse_ref, wind_ref, part_ref, left_ref, right_ref, send_ref):
    level = place_ref[0] * 8 + place_ref[1]
    at_left = place_ref[2] == 0
    at_right = place_ref[2] == 3
    spread = (0.25 * STEP) * diffuse_ref[level]
    along_x = (0.5 * STEP) * wind_ref[0, level]
    along_y = (0.5 * STEP) * wind_ref[1, level]

    lane = lanes(8)
    row = rows_of(8)
    column = lane % 16
    zero = jnp.zeros((8, W), F32)

    def neighbours(tile):
        up = jnp.where(row < 7, pltpu.roll(tile, 7, 0), zero)
        down = jnp.where(row > 0, pltpu.roll(tile, 1, 0), zero)
        return up, down

    def along_rows(tile, up, down):
        east = pltpu.roll(jnp.where(lane < 16, up, tile), W - 16, 1)
        west = pltpu.roll(jnp.where(lane >= W - 16, down, tile), 16, 1)
        return east, west

    def along_columns(tiles):
        after = [pltpu.roll(tile, W - 1, 1) for tile in tiles]
        before = [pltpu.roll(tile, 1, 1) for tile in tiles]
        after_far = [pltpu.roll(tile, 15, 1) for tile in tiles[1:]] + [zero]
        before_far = [zero] + [pltpu.roll(tile, W - 15, 1) for tile in tiles[:-1]]
        north = [jnp.where(column < 15, near, far) for near, far in zip(after, after_far)]
        south = [jnp.where(column > 0, near, far) for near, far in zip(before, before_far)]
        return north, south

    def cleared(tiles):
        return [jnp.where(at_left, zero, tiles[0]), tiles[1], tiles[2], jnp.where(at_right, zero, tiles[3])]

    def part(n):
        return cleared(
            [
                left_ref[8 * n : 8 * n + 8, :],
                part_ref[pl.ds(16 * n, 8, stride=2), :],
                part_ref[pl.ds(16 * n + 1, 8, stride=2), :],
                right_ref[8 * n : 8 * n + 8, :],
            ]
        )

    item = lane % 64
    end_lane = jnp.where(item < 16, item + (W - 16), jnp.where(item < 32, item - 16, 0))
    side_lane = jnp.clip(jnp.where(item < 48, (item - 33) * 16 + 15, (item - 49) * 16), 0, W - 1)
    corner_lane = jnp.where(item < 40, W - 1, jnp.where(item < 45, 15, jnp.where(item < 52, W - 16, 0)))
    is_corner = (item == 32) | (item == 41) | (item == 48) | (item == 57)

    def picked(values, index):
        return jnp.take_along_axis(values, index, axis=1)

    for r in range(3):
        send_ref[pl.ds(r, 8, stride=3), :] = zero
    coarse = part(0)
    for n in range(1, 8):
        north, south = along_columns(coarse)
        image = []
        for b in range(4):
            east, west = along_rows(coarse[b], *neighbours(coarse[b]))
            slope = along_x * (east - west) + along_y * (north[b] - south[b])
            total = (east + west) + (north[b] + south[b])
            image.append(coarse[b] + (spread * (total - 4.0 * coarse[b]) - coarse[b] * slope))
        image = cleared(image)
        beside = [neighbours(tile) for tile in image]

        rows = []
        for b in (1, 2):
            ends = picked(jnp.where(lane >= 64, beside[b][1], beside[b][0]), end_lane)
            sides = picked(jnp.where(column == 15, image[b - 1], image[b + 1]), side_lane)
            corners = jnp.where(
                lane >= 64,
                jnp.where(column == 15, beside[b - 1][1], beside[b + 1][1]),
                jnp.where(column == 15, beside[b - 1][0], beside[b + 1][0]),
            )
            corners = picked(corners, corner_lane)
            rows.append(jnp.where(item < 32, ends, jnp.where(is_corner, corners, sides)))
        base = n * 24
        send_ref[pl.ds(base, 8, stride=3), :] = image[1]
        send_ref[pl.ds(base + 1, 8, stride=3), :] = image[2]
        send_ref[pl.ds(base + 2, 8, stride=3), :] = jnp.where(lane < 64, rows[0], rows[1])

        if n < 7:
            blended = []
            for tile, pair in zip(image, beside):
                east, west = along_rows(tile, *pair)
                blended.append(BLEND[0] * west + BLEND[1] * tile + BLEND[2] * east)
            north, south = along_columns(blended)
            coarse = cleared(
                [
                    value + (BLEND[0] * s + BLEND[1] * tile + BLEND[2] * n_)
                    for value, s, tile, n_ in zip(part(n), south, blended, north)
                ]
            )


def base_kernel(end_ref, change_ref, base_ref, along_ref, fine_ref):
    lo = low(HALF)
    for j in range(CX):
        lower = change_ref[j * OROWS : (j + 1) * OROWS, :]
        middle = change_ref[(j + 1) * OROWS : (j + 2) * OROWS, :]
        upper = change_ref[(j + 2) * OROWS : (j + 3) * OROWS, :]
        for offset in range(4):
            along = WEIGHTS_MID[offset] * middle
            if offset < 2:
                along = along + WEIGHTS_LOW[offset] * lower
            else:
                along = along + WEIGHTS_HIGH[offset] * upper
            slot = offset * OROWS
            along_ref[slot : slot + OROWS, :] = along
            before = along_ref[slot : slot + CY, :]
            centre = along_ref[slot + 1 : slot + CY + 1, :]
            after = along_ref[slot + 2 : slot + CY + 2, :]
            for k in range(4):
                value = WEIGHTS_MID[k] * centre
                if k < 2:
                    value = value + WEIGHTS_LOW[k] * before
                else:
                    value = value + WEIGHTS_HIGH[k] * after
                fine_ref[pl.ds(offset * HALF + k, CY, stride=4), :] = value
        for pair in range(2):
            x = 4 * j + 2 * pair
            one = end_ref[x * HALF : (x + 1) * HALF, :] + fine_ref[2 * pair * HALF : (2 * pair + 1) * HALF, :]
            two = (
                end_ref[(x + 1) * HALF : (x + 2) * HALF, :]
                + fine_ref[(2 * pair + 1) * HALF : (2 * pair + 2) * HALF, :]
            )
            both = jnp.concatenate([jnp.where(lo, one, swap(two)), jnp.where(lo, swap(one), two)], axis=0).T
            base_ref[x * LEVELS : (x + 2) * LEVELS, :] = both


def column_weights():
    weights = np.zeros((3 * W, 10, W), np.float32)

    def put(k, j, cy):
        for offset in range(4):
            for at, factor in ((4 * (cy + 1), WEIGHTS_LOW), (4 * cy, WEIGHTS_MID), (4 * (cy - 1), WEIGHTS_HIGH)):
                if 0 <= at + offset < W:
                    weights[k, j, at + offset] += factor[offset]

    for h in range(2):
        for cx in range(CX):
            for c in range(CY):
                put(h * W + cx * CY + c, cx + 1, h * CY + c)
        for c in range(CY):
            put(2 * W + h * 64 + c, 0, h * CY + c)
            put(2 * W + h * 64 + CY + c, 9, h * CY + c)
        for j in range(10):
            if h == 0:
                put(2 * W + 32 + j, j, -1)
            else:
                put(2 * W + 64 + 48 + j, j, 2 * CY)
    return weights.reshape(3 * W, 10 * W).astype(ml_dtypes.bfloat16)


def end_kernel(base_ref, back_ref, weights_ref, out_ref, stage_ref, sem):
    values = jnp.concatenate([back_ref[pl.ds(r, LEVELS, stride=3), :] for r in range(3)], axis=1)
    first = values.astype(jnp.bfloat16)
    rest = values - first.astype(F32)
    second = rest.astype(jnp.bfloat16)
    third = (rest - second.astype(F32)).astype(jnp.bfloat16)
    stacked = jnp.concatenate([first, second, third], axis=0)
    columns = []
    copies = []
    for pair in range(5):
        product = jnp.dot(
            stacked, weights_ref[:, 2 * pair * W : 2 * (pair + 1) * W], preferred_element_type=F32
        )
        product = product[:LEVELS] + (product[LEVELS : 2 * LEVELS] + product[2 * LEVELS :])
        columns += [product[:, :W], product[:, W:]]
        if pair == 0:
            continue
        block = pair - 1
        for j in range(2 * block, 2 * block + 2):
            for offset in range(4):
                value = WEIGHTS_MID[offset] * columns[j + 1]
                if offset < 2:
                    value = value + WEIGHTS_LOW[offset] * columns[j]
                else:
                    value = value + WEIGHTS_HIGH[offset] * columns[j + 2]
                x = 4 * j + offset
                stage_ref[pl.ds(block * 8 * LEVELS + x % 8, LEVELS, stride=8), :] = (
                    base_ref[x * LEVELS : (x + 1) * LEVELS, :] + value
                )
        copy = pltpu.make_async_copy(
            stage_ref.reshape(4, LEVELS, 8, W).at[block], out_ref.at[:, pl.ds(8 * block, 8), :], sem.at[block]
        )
        copy.start()
        copies.append(copy)
    for copy in copies:
        copy.wait()


def shape(rows):
    return jax.ShapeDtypeStruct((rows, W), F32)


VMEM = pl.BlockSpec(memory_space=pltpu.VMEM)
SMEM = pl.BlockSpec(memory_space=pltpu.SMEM)
HBM = pl.BlockSpec(memory_space=pltpu.HBM)


def scratch(rows):
    return pltpu.VMEM((rows, W), F32)


def call(kernel, out_shape, in_specs, scratch_shapes, name, aliases=None, out_specs=None, cost=None, limit=24):
    many = isinstance(out_shape, tuple)
    return pl.pallas_call(
        kernel,
        out_shape=out_shape,
        in_specs=in_specs,
        out_specs=out_specs or ((VMEM,) * len(out_shape) if many else VMEM),
        scratch_shapes=scratch_shapes,
        input_output_aliases=aliases or {},
        cost_estimate=cost,
        compiler_params=pltpu.CompilerParams(vmem_limit_bytes=limit * 1024 * 1024),
        name=name,
    )


def ring(array, axis, distance):
    devices = lax.axis_size(axis)
    return lax.ppermute(array, axis, [(i, (i + distance) % devices) for i in range(devices)])


def shards(state_starts, diffusivity, wind):
    place = jnp.stack([lax.axis_index(axis) for axis in ("tm", "gx", "gy")]).astype(jnp.int32)
    field = state_starts.reshape(LEVELS, NX, W)
    edges, first_rows, last_rows = call(
        edge_kernel,
        (shape(16 * HALF), shape(STRIP), shape(STRIP)),
        [VMEM] * 2,
        [scratch(HALF)],
        "edges",
    )(field[:, :8].reshape(8 * LEVELS, W), field[:, NX - 8 :].reshape(8 * LEVELS, W))
    west = ring(last_rows, "gx", 1)
    east = ring(first_rows, "gx", -1)
    middle = call(
        middle_kernel,
        shape(16 * HALF),
        [VMEM],
        [],
        "middle",
        cost=pl.CostEstimate(flops=1 << 20, bytes_accessed=1 << 20, transcendentals=0),
    )(field[:, 8 : NX - 8].reshape(16 * LEVELS, W))
    first_columns, last_columns = call(side_kernel, (shape(SIDE), shape(SIDE)), [VMEM] * 4, [], "sides")(
        edges, middle, west, east
    )
    left = ring(last_columns, "gy", 1)
    right = ring(first_columns, "gy", -1)
    diffuse_row = diffusivity.reshape(1, LEVELS)
    states = (shape(40 * FROWS),) * 4 + (shape(NX * HALF), shape(12 * CROWS))
    inner = call(
        inner_kernel,
        states,
        [SMEM] + [VMEM] * 6,
        [scratch(FROWS)],
        "inner",
        cost=pl.CostEstimate(flops=1 << 24, bytes_accessed=8 << 20, transcendentals=0),
    )(place, edges, middle, west, east, diffuse_row, wind)
    outer = call(
        outer_kernel,
        states + (shape(10 * OROWS), shape(2 * LEVELS)),
        [SMEM] + [VMEM] * 12,
        [scratch(160 + CX * HALF), scratch(CX * OROWS), scratch(W)],
        "outer",
        aliases={7 + k: k for k in range(6)},
    )(place, west, east, left, right, diffuse_row, wind, *inner)
    fine_end, change, parts = outer[4], outer[6], outer[7]
    parts = lax.all_to_all(parts.reshape(LEVELS, 2, W), ("tm", "gx"), 0, 0, tiled=True).reshape(2 * LEVELS, W)
    first_half, second_half = call(split_kernel, (shape(LEVELS), shape(LEVELS)), [VMEM], [], "split")(parts)
    left = ring(second_half, "gy", 1)
    right = ring(first_half, "gy", -1)
    parts, fine_end = lax.optimization_barrier((parts, fine_end))
    base = call(
        base_kernel,
        shape(NX * LEVELS),
        [VMEM] * 2,
        [scratch(4 * OROWS), scratch(4 * HALF)],
        "base",
        cost=pl.CostEstimate(flops=1 << 22, bytes_accessed=2 << 20, transcendentals=0),
    )(fine_end, change)
    left, right, base = lax.optimization_barrier((left, right, base))
    images = call(chain_kernel, shape(3 * LEVELS), [SMEM] * 3 + [VMEM] * 3, [], "chain")(
        place, diffusivity, wind, parts, left, right
    )
    images = lax.all_to_all(images.reshape(LEVELS, 1, 3 * W), ("tm", "gx"), 0, 0, tiled=True)
    ending = call(
        end_kernel,
        jax.ShapeDtypeStruct((LEVELS, NX, W), F32),
        [VMEM] * 3,
        [scratch(NX * LEVELS), pltpu.SemaphoreType.DMA((4,))],
        "ending",
        out_specs=HBM,
    )(base, images.reshape(3 * LEVELS, W), jnp.asarray(column_weights()))
    return ending.reshape(1, LEVELS, NX, W)


def solution(mesh):
    placed = (P("tm", None, "gx", "gy"), P(), P())
    return jax.shard_map(
        shards, mesh=mesh, in_specs=placed, out_specs=P("tm", None, "gx", "gy"), check_vma=False
    )
```

time: 66 us -> 61.5 us (0.932)
  waiting for transfers between devices: 7.29 us -> 4.22 us
  blocking collectives: 38.8 us -> 37 us
    ppermute x6, waiting for transfers between devices: 7.29 us -> 4.22 us  [ring(): lax.ppermute(array, axis, [(i, (i + distance) % devices) for i in range(d...]
    unnamed x6 -> x8, local copies, waits for them, and re-layouts: 1.23 us -> 0.02 us
    reshape x2 -> x1, local copies, waits for them, and re-layouts: 0.09 us -> 1.16 us  [shards(): field[:, NX - 8:].reshape(8 * LEVELS, W)]
    all_to_all x1, blocking collectives: 22.3 us -> 21.4 us  [shards(): lax.all_to_all(parts.reshape(LEVELS, 2, W), ('tm', 'gx'), 0, 0, tiled=True)]
    all_to_all x1, blocking collectives: 16.4 us -> 15.6 us  [shards(): lax.all_to_all(images.reshape(LEVELS, 1, 3 * W), ('tm', 'gx'), 0, 0, tile...]
    pallas_call x4 -> x7, Pallas kernels: 7.43 us -> 7.78 us  [the longest x1 3.13 us: shards(): call(inner_kernel, states, [SMEM] + [VMEM] * 6, [scratch(FROWS)], 'inner'...]
  transfers between devices with their start and end apart: 6 -> 6, of which waited for: 5 -> 3; matrix products, arithmetic and copies ran while one was open for 0% -> 0% of each run, Pallas kernels for 0% -> 7%
where the time goes in v3:
time: 61.5 us; the launch traced here: 61.3 us
  blocking collectives  37 us (60%)
  Pallas kernels  10 us (16%)
  starting transfers between devices  8.7 us (14%)
  waiting for transfers between devices  4.22 us (7%)
  local copies, waits for them, and re-layouts  1.22 us (2%)
    all_to_all x1, blocking collectives, shards(): lax.all_to_all(parts.reshape(LEVELS, 2, W), ('tm', 'gx'), 0, 0, tiled=True)  21.4 us
    all_to_all x1, blocking collectives, shards(): lax.all_to_all(images.reshape(LEVELS, 1, 3 * W), ('tm', 'gx'), 0, 0, tile...  15.6 us
    ppermute x6, starting transfers between devices, ring(): lax.ppermute(array, axis, [(i, (i + distance) % devices) for i in range(d...  8.7 us
    ppermute x6, waiting for transfers between devices, ring(): lax.ppermute(array, axis, [(i, (i + distance) % devices) for i in range(d...  4.22 us
    pallas_call x1, Pallas kernels, shards(): call(inner_kernel, states, [SMEM] + [VMEM] * 6, [scratch(FROWS)], 'inner'...  3.13 us
    pallas_call x1, Pallas kernels, shards(): call(chain_kernel, shape(3 * LEVELS), [SMEM] * 3 + [VMEM] * 3, [], 'chain')  2.21 us
    pallas_call x1, Pallas kernels, shards(): call(outer_kernel, states + (shape(10 * OROWS), shape(2 * LEVELS)), [SMEM...  1.64 us
    pallas_call x1, Pallas kernels, shards(): call(end_kernel, jax.ShapeDtypeStruct((LEVELS, NX, W), F32), [VMEM] * 3,...  1.36 us
  transfers between devices with their start and end apart: 6, of which 3 were waited for; matrix products, arithmetic and copies ran while one was open for 0% of the time, Pallas kernels for 7%

profile of v3, /device:TPU:1, one launch (start us, length us, event | category | flops | bytes accessed | tf_op | source)
XLA Modules:
  0.0 61.3 jit_solution(8427033659536744841)
XLA Ops:
  0.0 0.0 copy-start.3
  0.0 1.2 %slice_bitcast_fusion = (f32[512,128]{1,0:T(8,128)S(1)}, f32[512,128]{1,0:T(8,128)S(1)}) fusion(f32[64,32,128]{2,1,0:T(8,128)} %bitcast.23), kind=kLoop, calls=%fused_computation | loop fusion | bytes 1048576 | tf_op jit(solution)/shard_map/reshape | solution.py:555
  1.2 0.4 edges.1
  1.6 0.0 copy-start.1
  1.6 0.0 copy-start.2
  1.6 2.6 %collective-permute-start = (f32[272,128]{1,0:T(8,128)S(1)}, f32[272,128]{1,0:T(8,128)S(1)}, u32[]{:S(2)}, u32[]{:S(2)}) collective-permute-start(f32[272,128]{1,0:T(8,128)S(1)} %get-tuple-element.26), channel_id=1, source_target_pairs={{0,4},{4,8},{8,12},{12,16},{16,20},{20,24},{24,28},{28,0},{1,5},{5... | collective-permute-start | bytes 417800 | tf_op jit(solution)/shard_map/ppermute | solution.py:543
  4.2 0.7 %collective-permute-start.1 = (f32[272,128]{1,0:T(8,128)S(1)}, f32[272,128]{1,0:T(8,128)S(1)}, u32[]{:S(2)}, u32[]{:S(2)}) collective-permute-start(f32[272,128]{1,0:T(8,128)S(1)} %get-tuple-element.27), channel_id=1, source_target_pairs={{0,28},{4,0},{8,4},{12,8},{16,12},{20,16},{24,20},{28,24},{1,29},{... | collective-permute-start | bytes 417800 | tf_op jit(solution)/shard_map/ppermute | solution.py:543
  4.9 0.0 copy-done.3
  4.9 0.4 middle.1.middle_ref
  5.3 0.9 %collective-permute-done.west_ref = f32[272,128]{1,0:T(8,128)S(1)} collective-permute-done((f32[272,128]{1,0:T(8,128)S(1)}, f32[272,128]{1,0:T(8,128)S(1)}, u32[]{:S(2)}, u32[]{:S(2)}) %collective-permute-start) | collective-permute-done | bytes 139296 | tf_op jit(solution)/shard_map/ppermute | solution.py:543
  6.2 2.8 %collective-permute-done.1.east_ref = f32[272,128]{1,0:T(8,128)S(1)} collective-permute-done((f32[272,128]{1,0:T(8,128)S(1)}, f32[272,128]{1,0:T(8,128)S(1)}, u32[]{:S(2)}, u32[]{:S(2)}) %collective-permute-start.1) | collective-permute-done | bytes 139296 | tf_op jit(solution)/shard_map/ppermute | solution.py:543
  9.0 0.1 sides.1
  9.1 1.1 %collective-permute-start.2 = (f32[168,128]{1,0:T(8,128)S(1)}, f32[168,128]{1,0:T(8,128)S(1)}, u32[]{:S(2)}, u32[]{:S(2)}) collective-permute-start(f32[168,128]{1,0:T(8,128)S(1)} %get-tuple-element.29), channel_id=1, source_target_pairs={{0,1},{1,2},{2,3},{3,0},{4,5},{5,6},{6,7},{7,4},{8,9},{9,10},{10,1... | collective-permute-start | bytes 258056 | tf_op jit(solution)/shard_map/ppermute | solution.py:543
  10.2 1.7 %collective-permute-start.3 = (f32[168,128]{1,0:T(8,128)S(1)}, f32[168,128]{1,0:T(8,128)S(1)}, u32[]{:S(2)}, u32[]{:S(2)}) collective-permute-start(f32[168,128]{1,0:T(8,128)S(1)} %get-tuple-element.30), channel_id=1, source_target_pairs={{0,3},{1,0},{2,1},{3,2},{4,7},{5,4},{6,5},{7,6},{8,11},{9,8},{10,9... | collective-permute-start | bytes 258056 | tf_op jit(solution)/shard_map/ppermute | solution.py:543
  11.9 0.1 pad_add_fusion.place_ref
  11.9 0.0 copy-done.1
  11.9 0.0 copy-done.2
  11.9 3.1 %inner.1 = (f32[3520,128]{1,0:T(8,128)S(1)}, f32[3520,128]{1,0:T(8,128)S(1)}, f32[3520,128]{1,0:T(8,128)S(1)}, f32[3520,128]{1,0:T(8,128)S(1)}, f32[2048,128]{1,0:T(8,128)S(1)}, /*index=5*/f32[480,128]{1,0:T(8,128)S(1)}) custom-call(s32[3]{0:T(128)S(1)} %pad_add_fusion.place_ref, f32[1024,128]{1,0:T(8,128)S(1)} %get-tuple-element.28.edge_ref, ...), custom_call_target="tpu_custom_call" | custom-call | flops 16777216 | bytes 8388608 | tf_op jit(solution)/shard_map/inner/pallas_call | solution.py:573
  15.1 0.0 collective-permute-done.2.left_ref
  15.1 0.0 collective-permute-done.3.right_ref
  15.1 1.6 %outer.1 = (f32[3520,128]{1,0:T(8,128)S(1)}, f32[3520,128]{1,0:T(8,128)S(1)}, f32[3520,128]{1,0:T(8,128)S(1)}, f32[3520,128]{1,0:T(8,128)S(1)}, f32[2048,128]{1,...) custom-call(s32[3]{0:T(128)S(1)} %pad_add_fusion.place_ref, ...), custom_call_target="tpu_custom_call", output_to_operand_aliasing={{0}: (7, {}), {1}: (8, {}), {2}: (9, {}), {3}: (10, {}), {4... | custom-call | tf_op jit(solution)/shard_map/outer/pallas_call | solution.py:581
  16.7 0.0 copy-start
  16.8 21.4 %all_to_all.10 = f32[64,2,128]{2,1,0:T(2,128)S(1)} all-to-all(f32[64,2,128]{2,1,0:T(2,128)S(1)} %bitcast.20), channel_id=1, replica_groups=mesh['tm'=8,'gx'=8,'gy'=4] {'tm','gx'}, dimensions={0} | all-to-all | bytes 131072 | tf_op jit(solution)/shard_map/all_to_all | solution.py:590
  38.2 1.0 %collective-permute-start.4 = (f32[64,128]{1,0:T(8,128)S(1)}, f32[64,128]{1,0:T(8,128)S(1)}, u32[]{:S(2)}, u32[]{:S(2)}) collective-permute-start(f32[64,128]{1,0:T(8,128)S(1)} %get-tuple-element.38), channel_id=1, source_target_pairs={{0,1},{1,2},{2,3},{3,0},{4,5},{5,6},{6,7},{7,4},{8,9},{9,10},{10,1... | collective-permute-start | bytes 98312 | tf_op jit(solution)/shard_map/ppermute | solution.py:543
  39.2 1.7 %collective-permute-start.5 = (f32[64,128]{1,0:T(8,128)S(1)}, f32[64,128]{1,0:T(8,128)S(1)}, u32[]{:S(2)}, u32[]{:S(2)}) collective-permute-start(f32[64,128]{1,0:T(8,128)S(1)} %get-tuple-element.39), channel_id=1, source_target_pairs={{0,3},{1,0},{2,1},{3,2},{4,7},{5,4},{6,5},{7,6},{8,11},{9,8},{10,9... | collective-permute-start | bytes 98312 | tf_op jit(solution)/shard_map/ppermute | solution.py:543
  40.8 0.7 %base.1.base_ref = f32[2048,128]{1,0:T(8,128)S(1)} custom-call(f32[2048,128]{1,0:T(8,128)S(1)} %get-tuple-element.41.end_ref, f32[240,128]{1,0:T(8,128)S(1)} %get-tuple-element.42.change_ref), custom_call_target="tpu_custom_call" | custom-call | flops 4194304 | bytes 2097152 | tf_op jit(solution)/shard_map/base/pallas_call | solution.py:595
  41.6 0.6 collective-permute-done.4.left_ref
  42.1 0.0 collective-permute-done.5.right_ref
  42.1 2.2 %chain.1 = f32[192,128]{1,0:T(8,128)S(1)} custom-call(s32[3]{0:T(128)S(1)} %pad_add_fusion.place_ref, f32[64]{0:T(128)S(1)} %copy-done.2, f32[2,64]{1,0:T(2,128)S(1)} %copy-done.1, f32[128,128]{1,0:T(8,128)S(1)} %bitcast.17, f32[64,128]{1,0:T(8,128)S(1)} %collective-permute-done.4.left_ref, f32[64,128]{1,0:T(8,128)S(1)} %collective-permute-done.5.right_ref), custom_call_target="tpu_custom_call" | custom-call | tf_op jit(solution)/shard_map/chain/pallas_call | solution.py:604
  44.4 15.6 %all_to_all.11 = f32[64,1,384]{2,1,0:T(1,128)S(1)} all-to-all(f32[64,1,384]{2,1,0:T(1,128)S(1)} %bitcast.19), channel_id=1, replica_groups=mesh['tm'=8,'gx'=8,'gy'=4] {'tm','gx'}, dimensions={0} | all-to-all | bytes 196608 | tf_op jit(solution)/shard_map/all_to_all | solution.py:607
  59.9 0.0 copy-done
  59.9 1.4 %ending.1 = f32[64,32,128]{2,1,0:T(8,128)} custom-call(f32[2048,128]{1,0:T(8,128)S(1)} %base.1.base_ref, f32[192,128]{1,0:T(8,128)S(1)} %bitcast.18, bf16[384,1280]{1,0:T(8,128)(2,1)S(1)} %copy-done), custom_call_target="tpu_custom_call" | custom-call | tf_op jit(solution)/shard_map/ending/pallas_call | solution.py:608
  (2 shorter events, 0.0 us)
Async XLA Ops:
  0.0 4.9 %copy-start.3 = (f32[1,64,32,128]{3,2,1,0:T(8,128)S(1)}, f32[1,64,32,128]{3,2,1,0:T(8,128)}, u32[]{:S(2)}) copy-start(f32[1,64,32,128]{3,2,1,0:T(8,128)} %param.4) | copy-start | bytes 3145732
  1.6 10.4 %copy-start.1 = (f32[2,64]{1,0:T(2,128)S(1)}, f32[2,64]{1,0:T(2,128)}, u32[]{:S(2)}) copy-start(f32[2,64]{1,0:T(2,128)} %wind_ref.5) | copy-start | bytes 1540
  1.6 10.4 %copy-start.2 = (f32[64]{0:T(128)S(1)}, f32[64]{0:T(128)}, u32[]{:S(2)}) copy-start(f32[64]{0:T(128)} %diffuse_ref.1) | copy-start | bytes 772
  1.6 4.6 %collective-permute-start = (f32[272,128]{1,0:T(8,128)S(1)}, f32[272,128]{1,0:T(8,128)S(1)}, u32[]{:S(2)}, u32[]{:S(2)}) collective-permute-start(f32[272,128]{1,0:T(8,128)S(1)} %get-tuple-element.26), channel_id=1, source_target_pairs={{0,4},{4,8},{8,12},{12,16},{16,20},{20,24},{24,28},{28,0},{1,5},{5... | collective-permute-start | bytes 417800 | tf_op jit(solution)/shard_map/ppermute | solution.py:543
  4.2 4.8 %collective-permute-start.1 = (f32[272,128]{1,0:T(8,128)S(1)}, f32[272,128]{1,0:T(8,128)S(1)}, u32[]{:S(2)}, u32[]{:S(2)}) collective-permute-start(f32[272,128]{1,0:T(8,128)S(1)} %get-tuple-element.27), channel_id=1, source_target_pairs={{0,28},{4,0},{8,4},{12,8},{16,12},{20,16},{24,20},{28,24},{1,29},{... | collective-permute-start | bytes 417800 | tf_op jit(solution)/shard_map/ppermute | solution.py:543
  9.1 6.0 %collective-permute-start.2 = (f32[168,128]{1,0:T(8,128)S(1)}, f32[168,128]{1,0:T(8,128)S(1)}, u32[]{:S(2)}, u32[]{:S(2)}) collective-permute-start(f32[168,128]{1,0:T(8,128)S(1)} %get-tuple-element.29), channel_id=1, source_target_pairs={{0,1},{1,2},{2,3},{3,0},{4,5},{5,6},{6,7},{7,4},{8,9},{9,10},{10,1... | collective-permute-start | bytes 258056 | tf_op jit(solution)/shard_map/ppermute | solution.py:543
  10.2 4.9 %collective-permute-start.3 = (f32[168,128]{1,0:T(8,128)S(1)}, f32[168,128]{1,0:T(8,128)S(1)}, u32[]{:S(2)}, u32[]{:S(2)}) collective-permute-start(f32[168,128]{1,0:T(8,128)S(1)} %get-tuple-element.30), channel_id=1, source_target_pairs={{0,3},{1,0},{2,1},{3,2},{4,7},{5,4},{6,5},{7,6},{8,11},{9,8},{10,9... | collective-permute-start | bytes 258056 | tf_op jit(solution)/shard_map/ppermute | solution.py:543
  16.7 43.2 %copy-start = (bf16[384,1280]{1,0:T(8,128)(2,1)S(1)}, bf16[384,1280]{1,0:T(8,128)(2,1)}, u32[]{:S(2)}) copy-start(bf16[384,1280]{1,0:T(8,128)(2,1)} %constant.15.clone.weights_ref) | copy-start | bytes 2949124
  38.2 4.0 %collective-permute-start.4 = (f32[64,128]{1,0:T(8,128)S(1)}, f32[64,128]{1,0:T(8,128)S(1)}, u32[]{:S(2)}, u32[]{:S(2)}) collective-permute-start(f32[64,128]{1,0:T(8,128)S(1)} %get-tuple-element.38), channel_id=1, source_target_pairs={{0,1},{1,2},{2,3},{3,0},{4,5},{5,6},{6,7},{7,4},{8,9},{9,10},{10,1... | collective-permute-start | bytes 98312 | tf_op jit(solution)/shard_map/ppermute | solution.py:543
  39.2 3.0 %collective-permute-start.5 = (f32[64,128]{1,0:T(8,128)S(1)}, f32[64,128]{1,0:T(8,128)S(1)}, u32[]{:S(2)}, u32[]{:S(2)}) collective-permute-start(f32[64,128]{1,0:T(8,128)S(1)} %get-tuple-element.39), channel_id=1, source_target_pairs={{0,3},{1,0},{2,1},{3,2},{4,7},{5,4},{6,5},{7,6},{8,11},{9,8},{10,9... | collective-permute-start | bytes 98312 | tf_op jit(solution)/shard_map/ppermute | solution.py:543

commit v4 on v3

--- a/solution.py
+++ b/solution.py
@@ -139,13 +139,13 @@
     return centre + ((factor * spread) * ((east + west) + (north + south) - 4.0 * centre) - centre * slope)
 
 
-def substeps(place_ref, states, end_ref, coefs, tiles, end_tiles):
-    at_west = place_ref[1] == 0
-    at_east = place_ref[1] == 7
+def substeps(states, end_ref, coefs, tiles, end_tiles):
+    at_west = lax.axis_index("gx") == 0
+    at_east = lax.axis_index("gx") == 7
     lo = low(8)
     zero8 = jnp.zeros((8, W), F32)
-    left_out = jnp.logical_and(place_ref[2] == 0, jnp.logical_and(rows_of(8) < 4, lo))
-    right_out = jnp.logical_and(place_ref[2] == 3, jnp.logical_and(rows_of(8) >= 4, jnp.logical_not(lo)))
+    left_out = jnp.logical_and(lax.axis_index("gy") == 0, jnp.logical_and(rows_of(8) < 4, lo))
+    right_out = jnp.logical_and(lax.axis_index("gy") == 3, jnp.logical_and(rows_of(8) >= 4, jnp.logical_not(lo)))
     for step in range(SUB - 1):
         for tile in tiles:
             for i in range(step + 1, 39 - step):
@@ -167,7 +167,7 @@
 
 
 def inner_kernel(
-    place_ref, edge_ref, middle_ref, west_ref, east_ref, diffuse_ref, wind_ref,
+    edge_ref, middle_ref, west_ref, east_ref, diffuse_ref, wind_ref,
     s0_ref, s1_ref, s2_ref, s3_ref, end_ref, coarse_ref, sum_ref,
 ):
     lo8 = low(8)
@@ -178,7 +178,7 @@
         before = jnp.where(lo8, zero8, swap(rows[HALF - 8 :]))
         after = jnp.where(lo8, swap(rows[:8]), zero8)
         if i < 4 or i >= 36:
-            outside = place_ref[1] == (0 if i < 4 else 7)
+            outside = lax.axis_index("gx") == (0 if i < 4 else 7)
             rows = jnp.where(outside, jnp.zeros_like(rows), rows)
             before = jnp.where(outside, zero8, before)
             after = jnp.where(outside, zero8, after)
@@ -199,21 +199,21 @@
         coarse_ref[start + 7 : start + 27, :] = coarse_rows(sum_ref, 4, 20)
 
     states = (s0_ref, s1_ref, s2_ref, s3_ref)
-    substeps(place_ref, states, end_ref, coefficients(diffuse_ref, wind_ref), range(9), range(8))
+    substeps(states, end_ref, coefficients(diffuse_ref, wind_ref), range(9), range(8))
 
 
 def outer_kernel(
-    place_ref, west_ref, east_ref, left_ref, right_ref, diffuse_ref, wind_ref,
+    west_ref, east_ref, left_ref, right_ref, diffuse_ref, wind_ref,
     s0_in, s1_in, s2_in, s3_in, end_in, coarse_in,
     s0_ref, s1_ref, s2_ref, s3_ref, end_ref, coarse_ref, change_ref, send_ref,
     sum_ref, blend_ref, part_ref,
 ):
     del s0_in, s1_in, s2_in, s3_in, end_in, coarse_in
-    first_segment = place_ref[0] == 0
-    at_west = place_ref[1] == 0
-    at_east = place_ref[1] == 7
-    at_left = place_ref[2] == 0
-    at_right = place_ref[2] == 3
+    first_segment = lax.axis_index("tm") == 0
+    at_west = lax.axis_index("gx") == 0
+    at_east = lax.axis_index("gx") == 7
+    at_left = lax.axis_index("gy") == 0
+    at_right = lax.axis_index("gy") == 3
     lo8 = low(8)
     zero8 = jnp.zeros((8, W), F32)
     coefs = coefficients(diffuse_ref, wind_ref)
@@ -285,7 +285,7 @@
             change_ref[o : o + 8, :] = jnp.where(first_segment, image, zero8) - image
 
     states = (s0_ref, s1_ref, s2_ref, s3_ref)
-    substeps(place_ref, states, end_ref, coefs, (0, 8), (0, 7))
+    substeps(states, end_ref, coefs, (0, 8), (0, 7))
 
     for j in range(CX):
         lower = change_ref[j * OROWS : (j + 1) * OROWS, :]
@@ -315,13 +315,12 @@
     second_ref[...] = part_ref[pl.ds(1, LEVELS, stride=2), :]
 
 
-def chain_kernel(place_ref, diffuse_ref, wind_ref, part_ref, left_ref, right_ref, send_ref):
-    level = place_ref[0] * 8 + place_ref[1]
-    at_left = place_ref[2] == 0
-    at_right = place_ref[2] == 3
-    spread = (0.25 * STEP) * diffuse_ref[level]
-    along_x = (0.5 * STEP) * wind_ref[0, level]
-    along_y = (0.5 * STEP) * wind_ref[1, level]
+def chain_kernel(level_ref, part_ref, left_ref, right_ref, send_ref):
+    at_left = lax.axis_index("gy") == 0
+    at_right = lax.axis_index("gy") == 3
+    spread = (0.25 * STEP) * level_ref[0:8, :]
+    along_x = (0.5 * STEP) * level_ref[8:16, :]
+    along_y = (0.5 * STEP) * level_ref[16:24, :]
 
     lane = lanes(8)
     row = rows_of(8)
@@ -515,7 +514,6 @@
 
 
 VMEM = pl.BlockSpec(memory_space=pltpu.VMEM)
-SMEM = pl.BlockSpec(memory_space=pltpu.SMEM)
 HBM = pl.BlockSpec(memory_space=pltpu.HBM)
 
 
@@ -544,7 +542,6 @@
 
 
 def shards(state_starts, diffusivity, wind):
-    place = jnp.stack([lax.axis_index(axis) for axis in ("tm", "gx", "gy")]).astype(jnp.int32)
     field = state_starts.reshape(LEVELS, NX, W)
     edges, first_rows, last_rows = call(
         edge_kernel,
@@ -568,24 +565,28 @@
     )
     left = ring(last_columns, "gy", 1)
     right = ring(first_columns, "gy", -1)
+    level = lax.axis_index("tm") * 8 + lax.axis_index("gx")
+    of_level = jnp.concatenate([diffusivity[None], wind], axis=0)
+    of_level = lax.dynamic_slice_in_dim(of_level, level, 1, axis=1)
+    of_level = jnp.broadcast_to(of_level[:, None, :], (3, 8, W)).reshape(24, W)
     diffuse_row = diffusivity.reshape(1, LEVELS)
     states = (shape(40 * FROWS),) * 4 + (shape(NX * HALF), shape(12 * CROWS))
     inner = call(
         inner_kernel,
         states,
-        [SMEM] + [VMEM] * 6,
+        [VMEM] * 6,
         [scratch(FROWS)],
         "inner",
         cost=pl.CostEstimate(flops=1 << 24, bytes_accessed=8 << 20, transcendentals=0),
-    )(place, edges, middle, west, east, diffuse_row, wind)
+    )(edges, middle, west, east, diffuse_row, wind)
     outer = call(
         outer_kernel,
         states + (shape(10 * OROWS), shape(2 * LEVELS)),
-        [SMEM] + [VMEM] * 12,
+        [VMEM] * 12,
         [scratch(160 + CX * HALF), scratch(CX * OROWS), scratch(W)],
         "outer",
-        aliases={7 + k: k for k in range(6)},
-    )(place, west, east, left, right, diffuse_row, wind, *inner)
+        aliases={6 + k: k for k in range(6)},
+    )(west, east, left, right, diffuse_row, wind, *inner)
     fine_end, change, parts = outer[4], outer[6], outer[7]
     parts = lax.all_to_all(parts.reshape(LEVELS, 2, W), ("tm", "gx"), 0, 0, tiled=True).reshape(2 * LEVELS, W)
     first_half, second_half = call(split_kernel, (shape(LEVELS), shape(LEVELS)), [VMEM], [], "split")(parts)
@@ -601,8 +602,8 @@
         cost=pl.CostEstimate(flops=1 << 22, bytes_accessed=2 << 20, transcendentals=0),
     )(fine_end, change)
     left, right, base = lax.optimization_barrier((left, right, base))
-    images = call(chain_kernel, shape(3 * LEVELS), [SMEM] * 3 + [VMEM] * 3, [], "chain")(
-        place, diffusivity, wind, parts, left, right
+    images = call(chain_kernel, shape(3 * LEVELS), [VMEM] * 4, [], "chain")(
+        of_level, parts, left, right
     )
     images = lax.all_to_all(images.reshape(LEVELS, 1, 3 * W), ("tm", "gx"), 0, 0, tiled=True)
     ending = call(

time: 61.5 us -> 60.4 us (0.982)
  Pallas kernels: 10 us -> 8.34 us
    pallas_call x3, Pallas kernels: 6.98 us -> 5.35 us  [the longest x1 2.58 us: shards(): call(inner_kernel, states, [VMEM] * 6, [scratch(FROWS)], 'inner', cost=pl...]
  transfers between devices with their start and end apart: 6 -> 6, of which waited for: 3 -> 4; matrix products, arithmetic and copies ran while one was open for 0% -> 1% of each run, Pallas kernels for 7% -> 6%
where the time goes in v4:
time: 60.4 us; the launch traced here: 60.3 us
  blocking collectives  37.5 us (62%)
  starting transfers between devices  8.7 us (14%)
  Pallas kernels  8.34 us (14%)
  waiting for transfers between devices  3.97 us (7%)
  local copies, waits for them, and re-layouts  1.63 us (3%)
    all_to_all x1, blocking collectives, shards(): lax.all_to_all(parts.reshape(LEVELS, 2, W), ('tm', 'gx'), 0, 0, tiled=True)  21.7 us
    all_to_all x1, blocking collectives, shards(): lax.all_to_all(images.reshape(LEVELS, 1, 3 * W), ('tm', 'gx'), 0, 0, tile...  15.8 us
    ppermute x6, starting transfers between devices, ring(): lax.ppermute(array, axis, [(i, (i + distance) % devices) for i in range(d...  8.7 us
    ppermute x6, waiting for transfers between devices, ring(): lax.ppermute(array, axis, [(i, (i + distance) % devices) for i in range(d...  3.97 us
    pallas_call x1, Pallas kernels, shards(): call(inner_kernel, states, [VMEM] * 6, [scratch(FROWS)], 'inner', cost=pl...  2.58 us
    pallas_call x1, Pallas kernels, shards(): call(chain_kernel, shape(3 * LEVELS), [VMEM] * 4, [], 'chain')  1.65 us
    pallas_call x1, Pallas kernels, shards(): call(end_kernel, jax.ShapeDtypeStruct((LEVELS, NX, W), F32), [VMEM] * 3,...  1.36 us
  transfers between devices with their start and end apart: 6, of which 4 were waited for; matrix products, arithmetic and copies ran while one was open for 1% of the time, Pallas kernels for 6%

profile of v4, /device:TPU:1, one launch (start us, length us, event | category | flops | bytes accessed | tf_op | source)
XLA Modules:
  0.0 60.3 jit_solution(16055110024003876609)
XLA Ops:
  0.0 1.2 %slice_bitcast_fusion = (f32[512,128]{1,0:T(8,128)S(1)}, f32[512,128]{1,0:T(8,128)S(1)}) fusion(f32[64,32,128]{2,1,0:T(8,128)} %bitcast.21), kind=kLoop, calls=%fused_computation | loop fusion | bytes 1048576 | tf_op jit(solution)/shard_map/reshape | solution.py:552
  1.2 0.4 edges.1
  1.6 0.0 copy-start.1
  1.6 0.0 copy-start.2
  1.6 2.6 %collective-permute-start = (f32[272,128]{1,0:T(8,128)S(1)}, f32[272,128]{1,0:T(8,128)S(1)}, u32[]{:S(2)}, u32[]{:S(2)}) collective-permute-start(f32[272,128]{1,0:T(8,128)S(1)} %get-tuple-element.26), channel_id=1, source_target_pairs={{0,4},{4,8},{8,12},{12,16},{16,20},{20,24},{24,28},{28,0},{1,5},{5... | collective-permute-start | bytes 417800 | tf_op jit(solution)/shard_map/ppermute | solution.py:541
  4.2 0.7 %collective-permute-start.1 = (f32[272,128]{1,0:T(8,128)S(1)}, f32[272,128]{1,0:T(8,128)S(1)}, u32[]{:S(2)}, u32[]{:S(2)}) collective-permute-start(f32[272,128]{1,0:T(8,128)S(1)} %get-tuple-element.27), channel_id=1, source_target_pairs={{0,28},{4,0},{8,4},{12,8},{16,12},{20,16},{24,20},{28,24},{1,29},{... | collective-permute-start | bytes 417800 | tf_op jit(solution)/shard_map/ppermute | solution.py:541
  4.9 0.0 copy-done.3
  4.9 0.4 middle.1.middle_ref
  5.3 0.9 %collective-permute-done.west_ref = f32[272,128]{1,0:T(8,128)S(1)} collective-permute-done((f32[272,128]{1,0:T(8,128)S(1)}, f32[272,128]{1,0:T(8,128)S(1)}, u32[]{:S(2)}, u32[]{:S(2)}) %collective-permute-start) | collective-permute-done | bytes 139296 | tf_op jit(solution)/shard_map/ppermute | solution.py:541
  6.2 2.8 %collective-permute-done.1.east_ref = f32[272,128]{1,0:T(8,128)S(1)} collective-permute-done((f32[272,128]{1,0:T(8,128)S(1)}, f32[272,128]{1,0:T(8,128)S(1)}, u32[]{:S(2)}, u32[]{:S(2)}) %collective-permute-start.1) | collective-permute-done | bytes 139296 | tf_op jit(solution)/shard_map/ppermute | solution.py:541
  9.0 0.1 sides.1
  9.1 1.1 %collective-permute-start.2 = (f32[168,128]{1,0:T(8,128)S(1)}, f32[168,128]{1,0:T(8,128)S(1)}, u32[]{:S(2)}, u32[]{:S(2)}) collective-permute-start(f32[168,128]{1,0:T(8,128)S(1)} %get-tuple-element.29), channel_id=1, source_target_pairs={{0,1},{1,2},{2,3},{3,0},{4,5},{5,6},{6,7},{7,4},{8,9},{9,10},{10,1... | collective-permute-start | bytes 258056 | tf_op jit(solution)/shard_map/ppermute | solution.py:541
  10.2 1.7 %collective-permute-start.3 = (f32[168,128]{1,0:T(8,128)S(1)}, f32[168,128]{1,0:T(8,128)S(1)}, u32[]{:S(2)}, u32[]{:S(2)}) collective-permute-start(f32[168,128]{1,0:T(8,128)S(1)} %get-tuple-element.30), channel_id=1, source_target_pairs={{0,3},{1,0},{2,1},{3,2},{4,7},{5,4},{6,5},{7,6},{8,11},{9,8},{10,9... | collective-permute-start | bytes 258056 | tf_op jit(solution)/shard_map/ppermute | solution.py:541
  11.9 0.0 copy-done.1
  11.9 2.6 %inner.1 = (f32[3520,128]{1,0:T(8,128)S(1)}, f32[3520,128]{1,0:T(8,128)S(1)}, f32[3520,128]{1,0:T(8,128)S(1)}, f32[3520,128]{1,0:T(8,128)S(1)}, f32[2048,128]{1,0:T(8,128)S(1)}, /*index=5*/f32[480,128]{1,0:T(8,128)S(1)}) custom-call(f32[1024,128]{1,0:T(8,128)S(1)} %get-tuple-element.28.edge_ref, f32[1024,128]{1,0:T(8,128)S(1)} %middle.1.middle_ref, ...), custom_call_target="tpu_custom_call" | custom-call | flops 16777216 | bytes 8388608 | tf_op jit(solution)/shard_map/inner/pallas_call | solution.py:574
  14.5 0.0 collective-permute-done.2.left_ref
  14.5 0.0 collective-permute-done.3.right_ref
  14.5 1.1 %outer.1 = (f32[3520,128]{1,0:T(8,128)S(1)}, f32[3520,128]{1,0:T(8,128)S(1)}, f32[3520,128]{1,0:T(8,128)S(1)}, f32[3520,128]{1,0:T(8,128)S(1)}, f32[2048,128]{1,...) custom-call(f32[272,128]{1,0:T(8,128)S(1)} %collective-permute-done., ...), custom_call_target="tpu_custom_call", output_to_operand_aliasing={{0}: (6, {}), {1}: (7, {}), {2}: (8, {}), {3}: (9, {}), {4}... | custom-call | tf_op jit(solution)/shard_map/outer/pallas_call | solution.py:582
  15.6 0.0 copy-start
  15.6 21.7 %all_to_all.10 = f32[64,2,128]{2,1,0:T(2,128)S(1)} all-to-all(f32[64,2,128]{2,1,0:T(2,128)S(1)} %bitcast.17), channel_id=1, replica_groups=mesh['tm'=8,'gx'=8,'gy'=4] {'tm','gx'}, dimensions={0} | all-to-all | bytes 131072 | tf_op jit(solution)/shard_map/all_to_all | solution.py:591
  37.3 1.3 %collective-permute-start.4 = (f32[64,128]{1,0:T(8,128)S(1)}, f32[64,128]{1,0:T(8,128)S(1)}, u32[]{:S(2)}, u32[]{:S(2)}) collective-permute-start(f32[64,128]{1,0:T(8,128)S(1)} %get-tuple-element.38), channel_id=1, source_target_pairs={{0,1},{1,2},{2,3},{3,0},{4,5},{5,6},{6,7},{7,4},{8,9},{9,10},{10,1... | collective-permute-start | bytes 98312 | tf_op jit(solution)/shard_map/ppermute | solution.py:541
  38.6 1.4 %collective-permute-start.5 = (f32[64,128]{1,0:T(8,128)S(1)}, f32[64,128]{1,0:T(8,128)S(1)}, u32[]{:S(2)}, u32[]{:S(2)}) collective-permute-start(f32[64,128]{1,0:T(8,128)S(1)} %get-tuple-element.39), channel_id=1, source_target_pairs={{0,3},{1,0},{2,1},{3,2},{4,7},{5,4},{6,5},{7,6},{8,11},{9,8},{10,9... | collective-permute-start | bytes 98312 | tf_op jit(solution)/shard_map/ppermute | solution.py:541
  40.0 0.2 dynamic-slice_reduce_fusion
  40.2 0.1 broadcast_in_dim.14
  40.3 0.1 broadcast_in_dim.15
  40.4 0.7 %base.1.base_ref = f32[2048,128]{1,0:T(8,128)S(1)} custom-call(f32[2048,128]{1,0:T(8,128)S(1)} %get-tuple-element.41.end_ref, f32[240,128]{1,0:T(8,128)S(1)} %get-tuple-element.42.change_ref), custom_call_target="tpu_custom_call" | custom-call | flops 4194304 | bytes 2097152 | tf_op jit(solution)/shard_map/base/pallas_call | solution.py:596
  41.1 0.2 collective-permute-done.4.left_ref
  41.3 0.1 collective-permute-done.5.right_ref
  41.4 0.1 broadcast_in_dim.16.level_ref
  41.5 1.7 %chain.1 = f32[192,128]{1,0:T(8,128)S(1)} custom-call(f32[24,128]{1,0:T(8,128)S(1)} %broadcast_in_dim.16.level_ref, f32[128,128]{1,0:T(8,128)S(1)} %bitcast.14, f32[64,128]{1,0:T(8,128)S(1)} %collective-permute-done.4.left_ref, f32[64,128]{1,0:T(8,128)S(1)} %collective-permute-done.5.right_ref), custom_call_target="tpu_custom_call" | custom-call | tf_op jit(solution)/shard_map/chain/pallas_call | solution.py:605
  43.1 15.8 %all_to_all.11 = f32[64,1,384]{2,1,0:T(1,128)S(1)} all-to-all(f32[64,1,384]{2,1,0:T(1,128)S(1)} %bitcast.16), channel_id=1, replica_groups=mesh['tm'=8,'gx'=8,'gy'=4] {'tm','gx'}, dimensions={0} | all-to-all | bytes 196608 | tf_op jit(solution)/shard_map/all_to_all | solution.py:608
  58.9 1.4 %ending.1 = f32[64,32,128]{2,1,0:T(8,128)} custom-call(f32[2048,128]{1,0:T(8,128)S(1)} %base.1.base_ref, f32[192,128]{1,0:T(8,128)S(1)} %bitcast.15, bf16[384,1280]{1,0:T(8,128)(2,1)S(1)} %copy-done), custom_call_target="tpu_custom_call" | custom-call | tf_op jit(solution)/shard_map/ending/pallas_call | solution.py:609
  (6 shorter events, 0.1 us)
Async XLA Ops:
  0.0 4.9 %copy-start.3 = (f32[1,64,32,128]{3,2,1,0:T(8,128)S(1)}, f32[1,64,32,128]{3,2,1,0:T(8,128)}, u32[]{:S(2)}) copy-start(f32[1,64,32,128]{3,2,1,0:T(8,128)} %param.4) | copy-start | bytes 3145732
  1.6 10.3 %copy-start.1 = (f32[2,64]{1,0:T(2,128)S(1)}, f32[2,64]{1,0:T(2,128)}, u32[]{:S(2)}) copy-start(f32[2,64]{1,0:T(2,128)} %wind_ref.3) | copy-start | bytes 1540
  1.6 10.3 %copy-start.2 = (f32[64]{0:T(128)S(1)}, f32[64]{0:T(128)}, u32[]{:S(2)}) copy-start(f32[64]{0:T(128)} %param.5) | copy-start | bytes 772
  1.6 4.6 %collective-permute-start = (f32[272,128]{1,0:T(8,128)S(1)}, f32[272,128]{1,0:T(8,128)S(1)}, u32[]{:S(2)}, u32[]{:S(2)}) collective-permute-start(f32[272,128]{1,0:T(8,128)S(1)} %get-tuple-element.26), channel_id=1, source_target_pairs={{0,4},{4,8},{8,12},{12,16},{16,20},{20,24},{24,28},{28,0},{1,5},{5... | collective-permute-start | bytes 417800 | tf_op jit(solution)/shard_map/ppermute | solution.py:541
  4.2 4.8 %collective-permute-start.1 = (f32[272,128]{1,0:T(8,128)S(1)}, f32[272,128]{1,0:T(8,128)S(1)}, u32[]{:S(2)}, u32[]{:S(2)}) collective-permute-start(f32[272,128]{1,0:T(8,128)S(1)} %get-tuple-element.27), channel_id=1, source_target_pairs={{0,28},{4,0},{8,4},{12,8},{16,12},{20,16},{24,20},{28,24},{1,29},{... | collective-permute-start | bytes 417800 | tf_op jit(solution)/shard_map/ppermute | solution.py:541
  9.1 5.4 %collective-permute-start.2 = (f32[168,128]{1,0:T(8,128)S(1)}, f32[168,128]{1,0:T(8,128)S(1)}, u32[]{:S(2)}, u32[]{:S(2)}) collective-permute-start(f32[168,128]{1,0:T(8,128)S(1)} %get-tuple-element.29), channel_id=1, source_target_pairs={{0,1},{1,2},{2,3},{3,0},{4,5},{5,6},{6,7},{7,4},{8,9},{9,10},{10,1... | collective-permute-start | bytes 258056 | tf_op jit(solution)/shard_map/ppermute | solution.py:541
  10.2 4.3 %collective-permute-start.3 = (f32[168,128]{1,0:T(8,128)S(1)}, f32[168,128]{1,0:T(8,128)S(1)}, u32[]{:S(2)}, u32[]{:S(2)}) collective-permute-start(f32[168,128]{1,0:T(8,128)S(1)} %get-tuple-element.30), channel_id=1, source_target_pairs={{0,3},{1,0},{2,1},{3,2},{4,7},{5,4},{6,5},{7,6},{8,11},{9,8},{10,9... | collective-permute-start | bytes 258056 | tf_op jit(solution)/shard_map/ppermute | solution.py:541
  15.6 43.3 %copy-start = (bf16[384,1280]{1,0:T(8,128)(2,1)S(1)}, bf16[384,1280]{1,0:T(8,128)(2,1)}, u32[]{:S(2)}) copy-start(bf16[384,1280]{1,0:T(8,128)(2,1)} %constant.18.clone.weights_ref) | copy-start | bytes 2949124
  37.3 4.0 %collective-permute-start.4 = (f32[64,128]{1,0:T(8,128)S(1)}, f32[64,128]{1,0:T(8,128)S(1)}, u32[]{:S(2)}, u32[]{:S(2)}) collective-permute-start(f32[64,128]{1,0:T(8,128)S(1)} %get-tuple-element.38), channel_id=1, source_target_pairs={{0,1},{1,2},{2,3},{3,0},{4,5},{5,6},{6,7},{7,4},{8,9},{9,10},{10,1... | collective-permute-start | bytes 98312 | tf_op jit(solution)/shard_map/ppermute | solution.py:541
  38.6 2.8 %collective-permute-start.5 = (f32[64,128]{1,0:T(8,128)S(1)}, f32[64,128]{1,0:T(8,128)S(1)}, u32[]{:S(2)}, u32[]{:S(2)}) collective-permute-start(f32[64,128]{1,0:T(8,128)S(1)} %get-tuple-element.39), channel_id=1, source_target_pairs={{0,3},{1,0},{2,1},{3,2},{4,7},{5,4},{6,5},{7,6},{8,11},{9,8},{10,9... | collective-permute-start | bytes 98312 | tf_op jit(solution)/shard_map/ppermute | solution.py:541

commit v5 on v4

--- a/solution.py
+++ b/solution.py
@@ -166,38 +166,51 @@
             end_ref[o : o + 8, :] = advanced(states[SUB - 1], i * FROWS + 12 + 8 * tile, FROWS, coefs, 1.0)
 
 
+def laid(i, rows, outside, state_ref):
+    lo8 = low(8)
+    zero8 = jnp.zeros((8, W), F32)
+    before = jnp.where(lo8, zero8, swap(rows[HALF - 8 :]))
+    after = jnp.where(lo8, swap(rows[:8]), zero8)
+    if outside is not None:
+        rows = jnp.where(outside, jnp.zeros_like(rows), rows)
+        before = jnp.where(outside, zero8, before)
+        after = jnp.where(outside, zero8, after)
+    start = i * FROWS
+    state_ref[start : start + 4, :] = zero8[:4]
+    state_ref[start + 4 : start + 12, :] = before
+    state_ref[start + 12 : start + 76, :] = rows
+    state_ref[start + 76 : start + 84, :] = after
+    state_ref[start + 84 : start + 88, :] = zero8[:4]
+
+
+def coarsened(j, state_ref, coarse_ref, sum_ref):
+    base = 4 * j * FROWS
+    sum_ref[...] = (state_ref[base : base + FROWS, :] + state_ref[base + FROWS : base + 2 * FROWS, :]) + (
+        state_ref[base + 2 * FROWS : base + 3 * FROWS, :] + state_ref[base + 3 * FROWS : base + 4 * FROWS, :]
+    )
+    start = (j + 1) * CROWS
+    coarse_ref[start + 7 : start + 27, :] = coarse_rows(sum_ref, 4, 20)
+
+
+def block_kernel(edge_ref, middle_ref, s0_ref, coarse_ref, sum_ref):
+    for i in range(4, 36):
+        source, base = block_row(i - 4, edge_ref, middle_ref, None, None)
+        laid(i, source[base : base + HALF, :], None, s0_ref)
+    coarse_ref[...] = jnp.zeros_like(coarse_ref)
+    for j in range(1, 9):
+        coarsened(j, s0_ref, coarse_ref, sum_ref)
+
+
 def inner_kernel(
-    edge_ref, middle_ref, west_ref, east_ref, diffuse_ref, wind_ref,
+    west_ref, east_ref, diffuse_ref, wind_ref, s0_in, coarse_in,
     s0_ref, s1_ref, s2_ref, s3_ref, end_ref, coarse_ref, sum_ref,
 ):
-    lo8 = low(8)
-    zero8 = jnp.zeros((8, W), F32)
-    for i in range(40):
-        source, base = block_row(i - 4, edge_ref, middle_ref, west_ref, east_ref)
-        rows = source[base : base + HALF, :]
-        before = jnp.where(lo8, zero8, swap(rows[HALF - 8 :]))
-        after = jnp.where(lo8, swap(rows[:8]), zero8)
-        if i < 4 or i >= 36:
-            outside = lax.axis_index("gx") == (0 if i < 4 else 7)
-            rows = jnp.where(outside, jnp.zeros_like(rows), rows)
-            before = jnp.where(outside, zero8, before)
-            after = jnp.where(outside, zero8, after)
-        start = i * FROWS
-        s0_ref[start : start + 4, :] = zero8[:4]
-        s0_ref[start + 4 : start + 12, :] = before
-        s0_ref[start + 12 : start + 76, :] = rows
-        s0_ref[start + 76 : start + 84, :] = after
-        s0_ref[start + 84 : start + 88, :] = zero8[:4]
-
-    coarse_ref[...] = jnp.zeros_like(coarse_ref)
-    for j in range(10):
-        base = 4 * j * FROWS
-        sum_ref[...] = (s0_ref[base : base + FROWS, :] + s0_ref[base + FROWS : base + 2 * FROWS, :]) + (
-            s0_ref[base + 2 * FROWS : base + 3 * FROWS, :] + s0_ref[base + 3 * FROWS : base + 4 * FROWS, :]
-        )
-        start = (j + 1) * CROWS
-        coarse_ref[start + 7 : start + 27, :] = coarse_rows(sum_ref, 4, 20)
-
+    del s0_in, coarse_in
+    for i in (*range(4), *range(36, 40)):
+        source, base = block_row(i - 4, None, None, west_ref, east_ref)
+        laid(i, source[base : base + HALF, :], lax.axis_index("gx") == (0 if i < 4 else 7), s0_ref)
+    coarsened(0, s0_ref, coarse_ref, sum_ref)
+    coarsened(9, s0_ref, coarse_ref, sum_ref)
     states = (s0_ref, s1_ref, s2_ref, s3_ref)
     substeps(states, end_ref, coefficients(diffuse_ref, wind_ref), range(9), range(8))
 
@@ -560,8 +573,19 @@
         "middle",
         cost=pl.CostEstimate(flops=1 << 20, bytes_accessed=1 << 20, transcendentals=0),
     )(field[:, 8 : NX - 8].reshape(16 * LEVELS, W))
+    block, coarse = call(
+        block_kernel,
+        (shape(40 * FROWS), shape(12 * CROWS)),
+        [VMEM] * 2,
+        [scratch(FROWS)],
+        "block",
+        cost=pl.CostEstimate(flops=1 << 20, bytes_accessed=1 << 20, transcendentals=0),
+    )(edges, middle)
     first_columns, last_columns = call(side_kernel, (shape(SIDE), shape(SIDE)), [VMEM] * 4, [], "sides")(
         edges, middle, west, east
+    )
+    first_columns, last_columns, block, coarse = lax.optimization_barrier(
+        (first_columns, last_columns, block, coarse)
     )
     left = ring(last_columns, "gy", 1)
     right = ring(first_columns, "gy", -1)
@@ -577,8 +601,9 @@
         [VMEM] * 6,
         [scratch(FROWS)],
         "inner",
+        aliases={4: 0, 5: 5},
         cost=pl.CostEstimate(flops=1 << 24, bytes_accessed=8 << 20, transcendentals=0),
-    )(edges, middle, west, east, diffuse_row, wind)
+    )(west, east, diffuse_row, wind, block, coarse)
     outer = call(
         outer_kernel,
         states + (shape(10 * OROWS), shape(2 * LEVELS)),

time: 60.4 us -> 60.4 us (level)
    pallas_call x1 -> x2, Pallas kernels: 2.58 us -> 2.65 us  [the longest x1 2.42 us: shards(): call(inner_kernel, states, [VMEM] * 6, [scratch(FROWS)], 'inner', aliases...]
where the time goes in v5:
time: 60.4 us; the launch traced here: 60.2 us
  blocking collectives  37.7 us (62%)
  starting transfers between devices  8.7 us (14%)
  Pallas kernels  8.4 us (14%)
  waiting for transfers between devices  3.72 us (6%)
  local copies, waits for them, and re-layouts  1.63 us (3%)
    all_to_all x1, blocking collectives, shards(): lax.all_to_all(parts.reshape(LEVELS, 2, W), ('tm', 'gx'), 0, 0, tiled=True)  21.9 us
    all_to_all x1, blocking collectives, shards(): lax.all_to_all(images.reshape(LEVELS, 1, 3 * W), ('tm', 'gx'), 0, 0, tile...  15.8 us
    ppermute x6, starting transfers between devices, ring(): lax.ppermute(array, axis, [(i, (i + distance) % devices) for i in range(d...  8.7 us
    ppermute x6, waiting for transfers between devices, ring(): lax.ppermute(array, axis, [(i, (i + distance) % devices) for i in range(d...  3.72 us
    pallas_call x1, Pallas kernels, shards(): call(inner_kernel, states, [VMEM] * 6, [scratch(FROWS)], 'inner', aliases...  2.42 us
    pallas_call x1, Pallas kernels, shards(): call(chain_kernel, shape(3 * LEVELS), [VMEM] * 4, [], 'chain')  1.65 us
    pallas_call x1, Pallas kernels, shards(): call(end_kernel, jax.ShapeDtypeStruct((LEVELS, NX, W), F32), [VMEM] * 3,...  1.36 us
  transfers between devices with their start and end apart: 6, of which 4 were waited for; matrix products, arithmetic and copies ran while one was open for 1% of the time, Pallas kernels for 6%

profile of v5, /device:TPU:1, one launch (start us, length us, event | category | flops | bytes accessed | tf_op | source)
XLA Modules:
  0.0 60.2 jit_solution(14156401614547837209)
XLA Ops:
  0.0 1.2 %slice_bitcast_fusion = (f32[512,128]{1,0:T(8,128)S(1)}, f32[512,128]{1,0:T(8,128)S(1)}) fusion(f32[64,32,128]{2,1,0:T(8,128)} %bitcast.21), kind=kLoop, calls=%fused_computation | loop fusion | bytes 1048576 | tf_op jit(solution)/shard_map/reshape | solution.py:565
  1.2 0.4 edges.1
  1.6 2.6 %collective-permute-start = (f32[272,128]{1,0:T(8,128)S(1)}, f32[272,128]{1,0:T(8,128)S(1)}, u32[]{:S(2)}, u32[]{:S(2)}) collective-permute-start(f32[272,128]{1,0:T(8,128)S(1)} %get-tuple-element.32), channel_id=1, source_target_pairs={{0,4},{4,8},{8,12},{12,16},{16,20},{20,24},{24,28},{28,0},{1,5},{5... | collective-permute-start | bytes 417800 | tf_op jit(solution)/shard_map/ppermute | solution.py:554
  4.2 0.7 %collective-permute-start.1 = (f32[272,128]{1,0:T(8,128)S(1)}, f32[272,128]{1,0:T(8,128)S(1)}, u32[]{:S(2)}, u32[]{:S(2)}) collective-permute-start(f32[272,128]{1,0:T(8,128)S(1)} %get-tuple-element.33), channel_id=1, source_target_pairs={{0,28},{4,0},{8,4},{12,8},{16,12},{20,16},{24,20},{28,24},{1,29},{... | collective-permute-start | bytes 417800 | tf_op jit(solution)/shard_map/ppermute | solution.py:554
  4.9 0.0 copy-done.3
  4.9 0.0 copy-start.1
  4.9 0.0 copy-start.2
  4.9 0.4 middle.1.middle_ref
  5.3 0.2 block.1
  5.6 0.7 %collective-permute-done.west_ref = f32[272,128]{1,0:T(8,128)S(1)} collective-permute-done((f32[272,128]{1,0:T(8,128)S(1)}, f32[272,128]{1,0:T(8,128)S(1)}, u32[]{:S(2)}, u32[]{:S(2)}) %collective-permute-start) | collective-permute-done | bytes 139296 | tf_op jit(solution)/shard_map/ppermute | solution.py:554
  6.2 2.8 %collective-permute-done.1.east_ref = f32[272,128]{1,0:T(8,128)S(1)} collective-permute-done((f32[272,128]{1,0:T(8,128)S(1)}, f32[272,128]{1,0:T(8,128)S(1)}, u32[]{:S(2)}, u32[]{:S(2)}) %collective-permute-start.1) | collective-permute-done | bytes 139296 | tf_op jit(solution)/shard_map/ppermute | solution.py:554
  9.0 0.1 sides.1
  9.1 1.1 %collective-permute-start.2 = (f32[168,128]{1,0:T(8,128)S(1)}, f32[168,128]{1,0:T(8,128)S(1)}, u32[]{:S(2)}, u32[]{:S(2)}) collective-permute-start(f32[168,128]{1,0:T(8,128)S(1)} %get-tuple-element.39), channel_id=1, source_target_pairs={{0,1},{1,2},{2,3},{3,0},{4,5},{5,6},{6,7},{7,4},{8,9},{9,10},{10,1... | collective-permute-start | bytes 258056 | tf_op jit(solution)/shard_map/ppermute | solution.py:554
  10.2 1.7 %collective-permute-start.3 = (f32[168,128]{1,0:T(8,128)S(1)}, f32[168,128]{1,0:T(8,128)S(1)}, u32[]{:S(2)}, u32[]{:S(2)}) collective-permute-start(f32[168,128]{1,0:T(8,128)S(1)} %get-tuple-element.40), channel_id=1, source_target_pairs={{0,3},{1,0},{2,1},{3,2},{4,7},{5,4},{6,5},{7,6},{8,11},{9,8},{10,9... | collective-permute-start | bytes 258056 | tf_op jit(solution)/shard_map/ppermute | solution.py:554
  11.8 2.4 %inner.1 = (f32[3520,128]{1,0:T(8,128)S(1)}, f32[3520,128]{1,0:T(8,128)S(1)}, f32[3520,128]{1,0:T(8,128)S(1)}, f32[3520,128]{1,0:T(8,128)S(1)}, f32[2048,128]{1,0:T(8,128)S(1)}, /*index=5*/f32[480,128]{1,0:T(8,128)S(1)}) custom-call(f32[272,128]{1,0:T(8,128)S(1)} %collective-permute-done.west_ref, ...), custom_call_target="tpu_custom_call", output_to_operand_aliasing={{0}: (4, {}), {5}: (5, {})} | custom-call | flops 16777216 | bytes 8388608 | tf_op jit(solution)/shard_map/inner/pallas_call | solution.py:598
  14.3 0.0 collective-permute-done.2.left_ref
  14.3 0.0 collective-permute-done.3.right_ref
  14.3 1.1 %outer.1 = (f32[3520,128]{1,0:T(8,128)S(1)}, f32[3520,128]{1,0:T(8,128)S(1)}, f32[3520,128]{1,0:T(8,128)S(1)}, f32[3520,128]{1,0:T(8,128)S(1)}, f32[2048,128]{1,...) custom-call(f32[272,128]{1,0:T(8,128)S(1)} %collective-permute-done., ...), custom_call_target="tpu_custom_call", output_to_operand_aliasing={{0}: (6, {}), {1}: (7, {}), {2}: (8, {}), {3}: (9, {}), {4}... | custom-call | tf_op jit(solution)/shard_map/outer/pallas_call | solution.py:607
  15.4 0.0 copy-start
  15.4 21.9 %all_to_all.10 = f32[64,2,128]{2,1,0:T(2,128)S(1)} all-to-all(f32[64,2,128]{2,1,0:T(2,128)S(1)} %bitcast.17), channel_id=1, replica_groups=mesh['tm'=8,'gx'=8,'gy'=4] {'tm','gx'}, dimensions={0} | all-to-all | bytes 131072 | tf_op jit(solution)/shard_map/all_to_all | solution.py:616
  37.3 1.3 %collective-permute-start.4 = (f32[64,128]{1,0:T(8,128)S(1)}, f32[64,128]{1,0:T(8,128)S(1)}, u32[]{:S(2)}, u32[]{:S(2)}) collective-permute-start(f32[64,128]{1,0:T(8,128)S(1)} %get-tuple-element.50), channel_id=1, source_target_pairs={{0,1},{1,2},{2,3},{3,0},{4,5},{5,6},{6,7},{7,4},{8,9},{9,10},{10,1... | collective-permute-start | bytes 98312 | tf_op jit(solution)/shard_map/ppermute | solution.py:554
  38.6 1.4 %collective-permute-start.5 = (f32[64,128]{1,0:T(8,128)S(1)}, f32[64,128]{1,0:T(8,128)S(1)}, u32[]{:S(2)}, u32[]{:S(2)}) collective-permute-start(f32[64,128]{1,0:T(8,128)S(1)} %get-tuple-element.51), channel_id=1, source_target_pairs={{0,3},{1,0},{2,1},{3,2},{4,7},{5,4},{6,5},{7,6},{8,11},{9,8},{10,9... | collective-permute-start | bytes 98312 | tf_op jit(solution)/shard_map/ppermute | solution.py:554
  40.0 0.2 dynamic-slice_reduce_fusion
  40.2 0.1 broadcast_in_dim.14
  40.3 0.1 broadcast_in_dim.15
  40.3 0.7 %base.1.base_ref = f32[2048,128]{1,0:T(8,128)S(1)} custom-call(f32[2048,128]{1,0:T(8,128)S(1)} %get-tuple-element.53.end_ref, f32[240,128]{1,0:T(8,128)S(1)} %get-tuple-element.54.change_ref), custom_call_target="tpu_custom_call" | custom-call | flops 4194304 | bytes 2097152 | tf_op jit(solution)/shard_map/base/pallas_call | solution.py:621
  41.1 0.2 collective-permute-done.4.left_ref
  41.3 0.1 collective-permute-done.5.right_ref
  41.4 0.1 broadcast_in_dim.16.level_ref
  41.4 1.7 %chain.1 = f32[192,128]{1,0:T(8,128)S(1)} custom-call(f32[24,128]{1,0:T(8,128)S(1)} %broadcast_in_dim.16.level_ref, f32[128,128]{1,0:T(8,128)S(1)} %bitcast.14, f32[64,128]{1,0:T(8,128)S(1)} %collective-permute-done.4.left_ref, f32[64,128]{1,0:T(8,128)S(1)} %collective-permute-done.5.right_ref), custom_call_target="tpu_custom_call" | custom-call | tf_op jit(solution)/shard_map/chain/pallas_call | solution.py:630
  43.1 15.8 %all_to_all.11 = f32[64,1,384]{2,1,0:T(1,128)S(1)} all-to-all(f32[64,1,384]{2,1,0:T(1,128)S(1)} %bitcast.16), channel_id=1, replica_groups=mesh['tm'=8,'gx'=8,'gy'=4] {'tm','gx'}, dimensions={0} | all-to-all | bytes 196608 | tf_op jit(solution)/shard_map/all_to_all | solution.py:633
  58.9 1.4 %ending.1 = f32[64,32,128]{2,1,0:T(8,128)} custom-call(f32[2048,128]{1,0:T(8,128)S(1)} %base.1.base_ref, f32[192,128]{1,0:T(8,128)S(1)} %bitcast.15, bf16[384,1280]{1,0:T(8,128)(2,1)S(1)} %copy-done), custom_call_target="tpu_custom_call" | custom-call | tf_op jit(solution)/shard_map/ending/pallas_call | solution.py:634
  (7 shorter events, 0.1 us)
Async XLA Ops:
  0.0 4.9 %copy-start.3 = (f32[1,64,32,128]{3,2,1,0:T(8,128)S(1)}, f32[1,64,32,128]{3,2,1,0:T(8,128)}, u32[]{:S(2)}) copy-start(f32[1,64,32,128]{3,2,1,0:T(8,128)} %param.4) | copy-start | bytes 3145732
  1.6 4.6 %collective-permute-start = (f32[272,128]{1,0:T(8,128)S(1)}, f32[272,128]{1,0:T(8,128)S(1)}, u32[]{:S(2)}, u32[]{:S(2)}) collective-permute-start(f32[272,128]{1,0:T(8,128)S(1)} %get-tuple-element.32), channel_id=1, source_target_pairs={{0,4},{4,8},{8,12},{12,16},{16,20},{20,24},{24,28},{28,0},{1,5},{5... | collective-permute-start | bytes 417800 | tf_op jit(solution)/shard_map/ppermute | solution.py:554
  4.2 4.8 %collective-permute-start.1 = (f32[272,128]{1,0:T(8,128)S(1)}, f32[272,128]{1,0:T(8,128)S(1)}, u32[]{:S(2)}, u32[]{:S(2)}) collective-permute-start(f32[272,128]{1,0:T(8,128)S(1)} %get-tuple-element.33), channel_id=1, source_target_pairs={{0,28},{4,0},{8,4},{12,8},{16,12},{20,16},{24,20},{28,24},{1,29},{... | collective-permute-start | bytes 417800 | tf_op jit(solution)/shard_map/ppermute | solution.py:554
  4.9 6.9 %copy-start.1 = (f32[2,64]{1,0:T(2,128)S(1)}, f32[2,64]{1,0:T(2,128)}, u32[]{:S(2)}) copy-start(f32[2,64]{1,0:T(2,128)} %wind_ref.3) | copy-start | bytes 1540
  4.9 6.9 %copy-start.2 = (f32[64]{0:T(128)S(1)}, f32[64]{0:T(128)}, u32[]{:S(2)}) copy-start(f32[64]{0:T(128)} %param.5) | copy-start | bytes 772
  9.1 5.2 %collective-permute-start.2 = (f32[168,128]{1,0:T(8,128)S(1)}, f32[168,128]{1,0:T(8,128)S(1)}, u32[]{:S(2)}, u32[]{:S(2)}) collective-permute-start(f32[168,128]{1,0:T(8,128)S(1)} %get-tuple-element.39), channel_id=1, source_target_pairs={{0,1},{1,2},{2,3},{3,0},{4,5},{5,6},{6,7},{7,4},{8,9},{9,10},{10,1... | collective-permute-start | bytes 258056 | tf_op jit(solution)/shard_map/ppermute | solution.py:554
  10.2 4.1 %collective-permute-start.3 = (f32[168,128]{1,0:T(8,128)S(1)}, f32[168,128]{1,0:T(8,128)S(1)}, u32[]{:S(2)}, u32[]{:S(2)}) collective-permute-start(f32[168,128]{1,0:T(8,128)S(1)} %get-tuple-element.40), channel_id=1, source_target_pairs={{0,3},{1,0},{2,1},{3,2},{4,7},{5,4},{6,5},{7,6},{8,11},{9,8},{10,9... | collective-permute-start | bytes 258056 | tf_op jit(solution)/shard_map/ppermute | solution.py:554
  15.4 43.5 %copy-start = (bf16[384,1280]{1,0:T(8,128)(2,1)S(1)}, bf16[384,1280]{1,0:T(8,128)(2,1)}, u32[]{:S(2)}) copy-start(bf16[384,1280]{1,0:T(8,128)(2,1)} %constant.18.clone.weights_ref) | copy-start | bytes 2949124
  37.3 4.0 %collective-permute-start.4 = (f32[64,128]{1,0:T(8,128)S(1)}, f32[64,128]{1,0:T(8,128)S(1)}, u32[]{:S(2)}, u32[]{:S(2)}) collective-permute-start(f32[64,128]{1,0:T(8,128)S(1)} %get-tuple-element.50), channel_id=1, source_target_pairs={{0,1},{1,2},{2,3},{3,0},{4,5},{5,6},{6,7},{7,4},{8,9},{9,10},{10,1... | collective-permute-start | bytes 98312 | tf_op jit(solution)/shard_map/ppermute | solution.py:554
  38.6 2.8 %collective-permute-start.5 = (f32[64,128]{1,0:T(8,128)S(1)}, f32[64,128]{1,0:T(8,128)S(1)}, u32[]{:S(2)}, u32[]{:S(2)}) collective-permute-start(f32[64,128]{1,0:T(8,128)S(1)} %get-tuple-element.51), channel_id=1, source_target_pairs={{0,3},{1,0},{2,1},{3,2},{4,7},{5,4},{6,5},{7,6},{8,11},{9,8},{10,9... | collective-permute-start | bytes 98312 | tf_op jit(solution)/shard_map/ppermute | solution.py:554
